TPU v7x, 32 devices: a whole 2x2x4 slice. The times are simulated.
32 devices in a mesh: depth: 2 (over core), tiles: 16 (over z, y, x).
Axes of the slice: x: 2, y: 2, z: 4, core: 2. Of those that a mesh axis runs over, the one named last changes fastest.
Arguments:
- transmission: float32 [4, 2, 16, 256, 256], P('depth', None, 'tiles'), may hold values from -0.4 to 1.3
- illumination: float32 [2, 256, 256], replicated, may hold values from -6 to 6
- fresnel_taps: float32 [2, 31], replicated, may hold values from -1 to 1
- intensity: float32 [16, 2, 256, 256], P('tiles'), may hold values from 0 to 2
- offsets: int32 [16, 2, 2], P('tiles'), may hold values from 0 to 255, as said below
- counts: int32 [16], P('tiles'), may hold values from 0 to 2, as said below
Outputs:
- object_gradient: float32 [4, 2, 16, 256, 256], P('depth', None, 'tiles')
Inputs may be any that keep to these rules, and one draw needn't show every extreme that they name: `offsets`: A tile in the last row of tiles has row offset 0 in every slot, and a tile in the last column of tiles has column offset 0 in every slot, so every patch lies inside the object. Slots j >= counts[t] of tile t are unused.
All inputs are finite; a program needn't handle non-finite values.
Results may differ from a plain program's by a relative error of at most 0.0003.
Values sent between devices are 32-bit elements; how exact they have to be, the bound alone decides.
A program may use at most 64 MiB of HBM per device.

v0:
```python
import math

import jax
import jax.numpy as jnp
from jax import lax
from jax.sharding import PartitionSpec as P

GX = 4


HIGHEST = lax.Precision.HIGHEST


def shifted(shard, axis, by):
    peers = lax.axis_size(axis)
    pairs = [(i, i + by) for i in range(peers) if 0 <= i + by < peers]
    return lax.ppermute(shard, axis, pairs)


def product(first, second):
    return jnp.matmul(first, second, precision=HIGHEST)


def left_apply(matrix_real, matrix_imag, field_real, field_imag):
    return (
        product(matrix_real, field_real) - product(matrix_imag, field_imag),
        product(matrix_imag, field_real) + product(matrix_real, field_imag),
    )


def right_apply(field_real, field_imag, matrix_real, matrix_imag):
    return (
        product(field_real, matrix_real) - product(field_imag, matrix_imag),
        product(field_real, matrix_imag) + product(field_imag, matrix_real),
    )


def band_tables(fresnel_taps, patch_side):
    tap_count = fresnel_taps.shape[1]
    half_taps = tap_count // 2
    row_index = lax.broadcasted_iota(jnp.int32, (patch_side, patch_side), 0)
    col_index = lax.broadcasted_iota(jnp.int32, (patch_side, patch_side), 1)
    lag_index = col_index - row_index + half_taps
    band_real = jnp.zeros((patch_side, patch_side), jnp.float32)
    band_imag = jnp.zeros((patch_side, patch_side), jnp.float32)
    for tap_index in range(tap_count):
        on_band = lag_index == tap_index
        band_real = band_real + jnp.where(on_band, fresnel_taps[0, tap_index], 0.0)
        band_imag = band_imag + jnp.where(on_band, fresnel_taps[1, tap_index], 0.0)
    return (band_real, band_imag)


def fourier_tables(patch_side):
    row_index = lax.broadcasted_iota(jnp.int32, (patch_side, patch_side), 0)
    col_index = lax.broadcasted_iota(jnp.int32, (patch_side, patch_side), 1)
    phase = (row_index * col_index % patch_side).astype(jnp.float32) * (2.0 * math.pi / patch_side)
    factor = 1.0 / math.sqrt(patch_side)
    return (jnp.cos(phase) * factor, -jnp.sin(phase) * factor)


def forward_block(wave, object_patches, band_real, band_imag):
    wave_real = wave[:, 0]
    wave_imag = wave[:, 1]
    saved_list = []
    for slice_index in range(object_patches.shape[1]):
        saved_list.append(jnp.stack([wave_real, wave_imag], 1))
        object_real = object_patches[:, slice_index, 0]
        object_imag = object_patches[:, slice_index, 1]
        mixed_real = wave_real * object_real - wave_imag * object_imag
        mixed_imag = wave_real * object_imag + wave_imag * object_real
        half_real, half_imag = left_apply(band_real, band_imag, mixed_real, mixed_imag)
        wave_real, wave_imag = right_apply(half_real, half_imag, band_real.T, band_imag.T)
    return (jnp.stack([wave_real, wave_imag], 1), jnp.stack(saved_list, 1))


def backward_block(seed, saved_waves, object_patches, band_real, band_imag):
    grad_real = seed[:, 0]
    grad_imag = seed[:, 1]
    slice_total = object_patches.shape[1]
    patch_grads = [None] * slice_total
    for slice_index in reversed(range(slice_total)):
        half_real, half_imag = left_apply(band_real.T, -band_imag.T, grad_real, grad_imag)
        mixed_real, mixed_imag = right_apply(half_real, half_imag, band_real, -band_imag)
        input_real = saved_waves[:, slice_index, 0]
        input_imag = saved_waves[:, slice_index, 1]
        object_real = object_patches[:, slice_index, 0]
        object_imag = object_patches[:, slice_index, 1]
        patch_grads[slice_index] = jnp.stack(
            [
                input_real * mixed_real + input_imag * mixed_imag,
                input_real * mixed_imag - input_imag * mixed_real,
            ],
            1,
        )
        grad_real = object_real * mixed_real + object_imag * mixed_imag
        grad_imag = object_real * mixed_imag - object_imag * mixed_real
    return (jnp.stack([grad_real, grad_imag], 1), jnp.stack(patch_grads, 1))


def far_field(exit_wave, measured, live_flags, fourier_real, fourier_imag):
    half_real, half_imag = left_apply(fourier_real, fourier_imag, exit_wave[:, 0], exit_wave[:, 1])
    spectrum_real, spectrum_imag = right_apply(half_real, half_imag, fourier_real, fourier_imag)
    misfit = (
        spectrum_real * spectrum_real + spectrum_imag * spectrum_imag - measured
    ) * live_flags[:, None, None]
    back_real, back_imag = left_apply(
        fourier_real, -fourier_imag, 2.0 * misfit * spectrum_real, 2.0 * misfit * spectrum_imag
    )
    result_real, result_imag = right_apply(back_real, back_imag, fourier_real, -fourier_imag)
    return jnp.stack([result_real, result_imag], 1)


def neighbour(block, offset_by):
    return shifted(block, "tiles", offset_by)


def local(transmission, illumination, fresnel_taps, intensity, offsets, counts):
    object_tile = transmission[:, :, 0]
    tile_side = object_tile.shape[-1]
    patch_side = illumination.shape[-1]
    layer_count = object_tile.shape[0]
    slot_count = offsets.shape[1]
    measured_all = intensity[0]
    corners = offsets[0]
    live_count = counts[0]
    live_flags = (jnp.arange(slot_count, dtype=jnp.int32) < live_count).astype(jnp.float32)
    right_tile = neighbour(object_tile, -1)
    upper_band = jnp.concatenate([object_tile, right_tile], -1)
    lower_band = neighbour(upper_band, -GX)
    extended = jnp.concatenate([upper_band, lower_band], -2)

    def extract(corner_pair):
        return lax.dynamic_slice(
            extended,
            (0, 0, corner_pair[0], corner_pair[1]),
            (layer_count, 2, patch_side, patch_side),
        )

    all_patches = jax.vmap(extract)(corners)
    band_real, band_imag = band_tables(fresnel_taps, patch_side)
    fourier_real, fourier_imag = fourier_tables(patch_side)
    batch_count = slot_count // slot_count
    chain_length = lax.axis_size("depth")
    depth_index = lax.axis_index("depth")
    round_count = chain_length + batch_count - 1
    probe_batch = jnp.broadcast_to(illumination[None], (slot_count, 2, patch_side, patch_side))
    saved_all = jnp.zeros((slot_count, layer_count, 2, patch_side, patch_side), jnp.float32)
    exits_all = jnp.zeros((slot_count, 2, patch_side, patch_side), jnp.float32)

    def down_round(round_index, carried):
        incoming, saved_now, exits_now = carried
        batch_index = round_index - depth_index
        first_slot = jnp.clip(batch_index, 0, batch_count - 1) * slot_count
        working = (batch_index >= 0) & (batch_index < batch_count) & (first_slot < live_count)
        wave = jnp.where(depth_index == 0, probe_batch, incoming)

        def advance(buffers):
            leaving, saved_waves = forward_block(wave, all_patches, band_real, band_imag)
            return (
                leaving,
                lax.dynamic_update_slice_in_dim(buffers[0], saved_waves, first_slot, 0),
                leaving,
            )

        def down_pass_along(buffers):
            return (wave, buffers[0], buffers[1])

        leaving, saved_now, exits_now = lax.cond(
            working, advance, down_pass_along, (saved_now, exits_now)
        )
        incoming = shifted(leaving, "depth", 1)
        return (incoming, saved_now, exits_now)

    unused_wave, saved_all, exits_all = lax.fori_loop(
        0, round_count, down_round, (probe_batch, saved_all, exits_all)
    )
    grads_all = jnp.zeros((slot_count, layer_count, 2, patch_side, patch_side), jnp.float32)

    def up_round(round_index, carried):
        incoming, grads_now = carried
        batch_index = round_index - (chain_length - 1 - depth_index)
        first_slot = jnp.clip(batch_index, 0, batch_count - 1) * slot_count
        working = (batch_index >= 0) & (batch_index < batch_count) & (first_slot < live_count)

        def retreat(grads_old):
            final_wave = exits_all
            seed = lax.cond(
                depth_index == chain_length - 1,
                lambda arriving: far_field(
                    final_wave, measured_all, live_flags, fourier_real, fourier_imag
                ),
                lambda arriving: arriving,
                incoming,
            )
            upward, patch_grads = backward_block(seed, saved_all, all_patches, band_real, band_imag)
            return (upward, lax.dynamic_update_slice_in_dim(grads_old, patch_grads, first_slot, 0))

        def up_pass_along(grads_old):
            return (incoming, grads_old)

        upward, grads_now = lax.cond(working, retreat, up_pass_along, grads_now)
        incoming = shifted(upward, "depth", -1)
        return (incoming, grads_now)

    zero_batch = jnp.zeros((slot_count, 2, patch_side, patch_side), jnp.float32)
    unused_grad, grads_all = lax.fori_loop(0, round_count, up_round, (zero_batch, grads_all))

    def deposit(slot_index, field):
        corner_pair = corners[slot_index]
        start_tuple = (0, 0, corner_pair[0], corner_pair[1])
        current = lax.dynamic_slice(field, start_tuple, (layer_count, 2, patch_side, patch_side))
        return lax.dynamic_update_slice(field, current + grads_all[slot_index], start_tuple)

    gathered = lax.fori_loop(
        0,
        slot_count,
        deposit,
        jnp.zeros((layer_count, 2, 2 * tile_side, 2 * tile_side), jnp.float32),
    )
    upper_rows = gathered[:, :, :tile_side, :] + neighbour(gathered[:, :, tile_side:, :], GX)
    own_tile = upper_rows[..., :tile_side] + neighbour(upper_rows[..., tile_side:], 1)
    return own_tile[:, :, None]


def solution(mesh):
    placed = (
        P("depth", None, "tiles", None, None),
        P(),
        P(),
        P("tiles", None, None, None),
        P("tiles", None, None),
        P("tiles"),
    )
    return jax.shard_map(
        local,
        mesh=mesh,
        in_specs=placed,
        out_specs=P("depth", None, "tiles", None, None),
        check_vma=False,
    )
```

profile of v0, /device:TPU:8, one launch (start us, length us, event | category | flops | bytes accessed | tf_op | source)
XLA Modules:
  0.0 370.7 jit_solution(14517122720893001951)
XLA Ops:
  0.0 4.4 %collective-permute-start.2 = (f32[2,2,256,256]{3,2,1,0:T(8,128)}, f32[2,2,256,256]{3,2,1,0:T(8,128)S(1)}, u32[]{:S(2)}, u32[]{:S(2)}) collective-permute-start(f32[2,2,256,256]{3,2,1,0:T(8,128)} %bitcast.450), channel_id=1, source_target_pairs={{1,0},{2,1},{3,2},{4,3},{5,4},{6,5},{7,6},{8,7},{9,8},{10,9},{11,1... | collective-permute-start | bytes 3145736 | tf_op jit(solution)/shard_map/ppermute | solution.py:17
  4.4 22.8 %collective-permute-done.2 = f32[2,2,256,256]{3,2,1,0:T(8,128)S(1)} collective-permute-done((f32[2,2,256,256]{3,2,1,0:T(8,128)}, f32[2,2,256,256]{3,2,1,0:T(8,128)S(1)}, u32[]{:S(2)}, u32[]{:S(2)}) %collective-permute-start.2) | collective-permute-done | bytes 1048608 | tf_op jit(solution)/shard_map/ppermute | solution.py:17
  27.1 2.9 pad_maximum_fusion.5
  35.0 19.8 %select_add_fusion = f32[256,256]{1,0:T(8,128)S(1)} fusion(f32[]{:T(128)} %bitcast.131, f32[]{:T(128)} %bitcast.130, f32[]{:T(128)} %bitcast.129, f32[]{:T(128)} %bitcast.128, f32[]{:T(128)} %bitcast.127, f32[]{:T(128)} %bitcast.126, f32[]{:T(128)} %bitcast.125, f32[]{:T(128)} %bitcast.124, f32[]{:T(128)} %bitcast.123, f32[]{:T(128)} %bitcast.122, ...), kind=kLoop, calls=%fused_computation.211 | loop fusion | flops 6160384 | bytes 262268 | tf_op jit(solution)/shard_map/add | solution.py:49
  54.8 19.8 %select_add_fusion.1 = f32[256,256]{1,0:T(8,128)S(1)} fusion(f32[]{:T(128)} %bitcast.100, f32[]{:T(128)} %bitcast.99, f32[]{:T(128)} %bitcast.98, f32[]{:T(128)} %bitcast.97, f32[]{:T(128)} %bitcast.96, f32[]{:T(128)} %bitcast.95, f32[]{:T(128)} %bitcast.94, f32[]{:T(128)} %bitcast.93, f32[]{:T(128)} %bitcast.92, f32[]{:T(128)} %bitcast.91, f32[]{:T(128)} %bitcast.90, ...), kind=kLoop, calls=%fused_computation.212 | loop fusion | flops 6160384 | bytes 262268 | tf_op jit(solution)/shard_map/add | solution.py:48
  74.8 3.9 %collective-permute-done.3 = f32[2,2,256,512]{3,2,1,0:T(8,128)} collective-permute-done((f32[2,2,256,512]{3,2,1,0:T(8,128)}, f32[2,2,256,512]{3,2,1,0:T(8,128)}, u32[]{:S(2)}, u32[]{:S(2)}) %collective-permute-start.3) | collective-permute-done | bytes 2097184 | tf_op jit(solution)/shard_map/ppermute | solution.py:17
  78.7 4.1 %pad_maximum_fusion.4 = f32[2,2,512,512]{3,2,1,0:T(8,128)} fusion(f32[2,2,256,512]{3,2,1,0:T(8,128)} %collective-permute-done.3, f32[2,2,256,256]{3,2,1,0:T(8,128)S(1)} %collective-permute-done.2, f32[2,2,256,256]{3,2,1,0:T(8,128)S(1)} %bitcast.452), kind=kLoop, calls=%fused_computation.206 | loop fusion | flops 2097152 | bytes 8388608 | tf_op jit(solution)/shard_map/concatenate | solution.py:130
  84.4 9.3 %while.57 = (s32[]{:T(128)}, f32[2,2,512,512]{3,2,1,0:T(8,128)}, s32[2,4]{1,0:T(2,128)S(1)}, f32[2,2,2,256,256]{4,3,0,2,1:T(8,128)}, s32[]{:T(128)}) while((s32[]{:T(128)}, f32[2,2,512,512]{3,2,1,0:T(8,128)}, s32[2,4]{1,0:T(2,128)S(1)}, f32[2,2,2,256,256]{4,3,0,2,1:T(8,128)}, s32[]{:T(128)}) %tuple.262), condition=%wide.while_cond, body=%wide.while_body.sunk | while | flops 2 | bytes 2098801 | solution.py:133
  85.0 4.0 %bitcast_dynamic-update-slice_fusion.2 = f32[2,2,2,256,256]{4,3,0,2,1:T(8,128)} fusion(f32[2,2,2,256,256]{4,3,0,2,1:T(8,128)} %get-tuple-element.1457, s32[]{:T(128)} %get-tuple-element.1454, f32[2,2,512,512]{3,2,1,0:T(8,128)} %get-tuple-element.1460, s32[]{:T(128)} %bitcast.445, s32[]{:T(128)} %bitcast.446), kind=kLoop, calls=%fused_computation.112.clone.1 | loop fusion | bytes 2098688 | tf_op jit(solution)/shard_map/vmap()/gather
  89.7 4.0 %bitcast_dynamic-update-slice_fusion.2 = f32[2,2,2,256,256]{4,3,0,2,1:T(8,128)} fusion(f32[2,2,2,256,256]{4,3,0,2,1:T(8,128)} %get-tuple-element.1457, s32[]{:T(128)} %get-tuple-element.1454, f32[2,2,512,512]{3,2,1,0:T(8,128)} %get-tuple-element.1460, s32[]{:T(128)} %bitcast.445, s32[]{:T(128)} %bitcast.446), kind=kLoop, calls=%fused_computation.112.clone.1 | loop fusion | bytes 2098688 | tf_op jit(solution)/shard_map/vmap()/gather
  95.4 60.4 %while.58 = (s32[]{:T(128)}, f32[2,2,256,256]{3,2,0,1:T(8,128)S(1)}, f32[2,2,2,256,256]{4,3,0,2,1:T(8,128)}, f32[2,2,256,256]{3,2,0,1:T(8,128)S(1)}, s32[]{:T(12...) while((s32[]{:T(128)}, ...), condition=%wide.region_3.4_spmd.clone, body=%wide.region_0.3_spmd.clone.sunk | while | flops 6446383104 | bytes 48234844 | solution.py:174
  97.4 24.1 %conditional.10 = ((f32[2,2,256,256]{3,2,0,1:T(8,128)}, f32[2,2,2,256,256]{4,3,0,2,1:T(8,128)}, f32[2,2,256,256]{3,2,0,1:T(8,128)S(1)})) conditional(s32[]{:T(128)} %convert_element_type.86, (f32[2,2,256,256]{3,2,0,1:T(8,128)}, f32[2,2,2,256,256]{4,3,0,2,1:T(8,128)}, f32[2,2,256,256]{3,2,0,1:T(8,128)S(1)}) %tuple.251, (f32[2,2,256,256]{3,2,0,1:T(8,128)}, ...), branch_computations={%region_1.1_spmd, %region_2.2_spmd} | conditional | flops 6446120960 | bytes 41418784 | solution.py:168
  127.0 26.4 %collective-permute-start = (f32[2,2,256,256]{3,2,0,1:T(8,128)}, f32[2,2,256,256]{3,2,0,1:T(8,128)S(1)}, u32[]{:S(2)}, u32[]{:S(2)}) collective-permute-start(f32[2,2,256,256]{3,2,0,1:T(8,128)} %get-tuple-element.1418), channel_id=1, source_target_pairs={{0,16},{1,17},{2,18},{3,19},{4,20},{5,21},{6,22},{7,23},{8,24},{9,... | collective-permute-start | bytes 3145736 | tf_op jit(solution)/shard_map/while/body/eval_jaxpr/ppermute | solution.py:17
  157.5 93.0 %while.59 = (s32[]{:T(128)}, f32[2,2,256,256]{3,2,0,1:T(8,128)S(1)}, f32[2,2,2,256,256]{4,3,0,2,1:T(8,128)}, s32[]{:T(128)}, s32[]{:T(128)}, /*index=5*/f32[2,2,...) while((s32[]{:T(128)}, ...), condition=%wide.region_9.10_spmd.clone.clone.clone, body=%wide.region_4.9_spmd.clone.clone.clone.sunk | while | flops 12894404608 | bytes 91226800 | solution.py:206
  180.2 37.4 %collective-permute-done.1 = f32[2,2,256,256]{3,2,0,1:T(8,128)} collective-permute-done((f32[2,2,256,256]{3,2,0,1:T(8,128)S(1)}, f32[2,2,256,256]{3,2,0,1:T(8,128)}, u32[]{:S(2)}, u32[]{:S(2)}) %collective-permute-start.1) | collective-permute-done | bytes 1048608 | tf_op jit(solution)/shard_map/while/body/eval_jaxpr/ppermute | solution.py:17
  220.3 24.0 %conditional.11 = ((f32[2,2,256,256]{3,2,0,1:T(8,128)S(1)}, f32[2,2,2,256,256]{4,3,0,2,1:T(8,128)})) conditional(s32[]{:T(128)} %convert_element_type.89, (f32[2,2,256,256]{3,2,0,1:T(8,128)S(1)}, f32[2,2,2,256,256]{4,3,0,2,1:T(8,128)}) %tuple.254, (f32[2,2,2,256,256]{4,3,0,2,1:T(8,128)}, s32[]{:T(128)}, f32[2,2,256,256]{3,2,0,1:T(8,128)S(1)}, ...), branch_computations={%region_5.5_spmd, %region_6.8_spmd.clone} | conditional | flops 12893487104 | bytes 84410648 | solution.py:201
  239.7 2.9 fusion.93
  245.6 3.4 collective-permute-done.1
  253.0 36.1 %while.56 = (s32[]{:T(128)}, f32[2,2,512,512]{3,2,1,0:T(8,128)}, s32[2,2]{1,0:T(2,128)S(1)}, f32[2,2,2,256,256]{4,3,0,2,1:T(8,128)}, s32[]{:T(128)}, /*index=5*/s32[]{:T(128)}, s32[]{:T(128)}) while((s32[]{:T(128)}, f32[2,2,512,512]{3,2,1,0:T(8,128)}, s32[2,2]{1,0:T(2,128)S(1)}, f32[2,2,2,256,256]{4,3,0,2,1:T(8,128)}, s32[]{:T(128)}, ...), condition=%wide.region_11.12_spmd, body=%wide.region_10.11_spmd.sunk | while | flops 262152 | bytes 5243077 | solution.py:214
  259.7 11.2 %dynamic_update_slice.10 = f32[2,2,512,512]{3,2,1,0:T(8,128)} dynamic-update-slice(f32[2,2,512,512]{3,2,1,0:T(8,128)} %get-tuple-element.1562, f32[2,2,256,256]{3,2,1,0:T(8,128)S(1)} %bitcast_add_fusion.2, s32[]{:T(128)} %constant.151.clone.1..sunk, s32[]{:T(128)} %constant.151.clone.1..sunk, s32[]{:T(128)S(6)} %select_n.427, s32[]{:T(128)S(6)} %select_n.428) | dynamic-update-slice | bytes 2097156 | tf_op jit(solution)/shard_map/while/body/eval_jaxpr/dynamic_update_slice | solution.py:212
  277.5 11.6 %dynamic_update_slice.10 = f32[2,2,512,512]{3,2,1,0:T(8,128)} dynamic-update-slice(f32[2,2,512,512]{3,2,1,0:T(8,128)} %get-tuple-element.1562, f32[2,2,256,256]{3,2,1,0:T(8,128)S(1)} %bitcast_add_fusion.2, s32[]{:T(128)} %constant.151.clone.1..sunk, s32[]{:T(128)} %constant.151.clone.1..sunk, s32[]{:T(128)S(6)} %select_n.427, s32[]{:T(128)S(6)} %select_n.428) | dynamic-update-slice | bytes 2097156 | tf_op jit(solution)/shard_map/while/body/eval_jaxpr/dynamic_update_slice | solution.py:212
  293.0 47.6 %collective-permute-done.4 = f32[2,2,256,512]{3,2,1,0:T(8,128)S(1)} collective-permute-done((f32[2,2,256,512]{3,2,1,0:T(8,128)S(1)}, f32[2,2,256,512]{3,2,1,0:T(8,128)S(1)}, u32[]{:S(2)}, u32[]{:S(2)}) %collective-permute-start.4) | collective-permute-done | bytes 2097184 | tf_op jit(solution)/shard_map/ppermute | solution.py:17
  341.2 4.3 %collective-permute-start.5 = (f32[2,2,256,256]{3,2,1,0:T(8,128)S(1)}, f32[2,2,256,256]{3,2,1,0:T(8,128)S(1)}, u32[]{:S(2)}, u32[]{:S(2)}) collective-permute-start(f32[2,2,256,256]{3,2,1,0:T(8,128)S(1)} %slice.397), channel_id=1, source_target_pairs={{0,1},{1,2},{2,3},{3,4},{4,5},{5,6},{6,7},{7,8},{8,9},{9,10},{10,1... | collective-permute-start | bytes 3145736 | tf_op jit(solution)/shard_map/ppermute | solution.py:17
  345.6 23.7 %collective-permute-done.5 = f32[2,2,256,256]{3,2,1,0:T(8,128)S(1)} collective-permute-done((f32[2,2,256,256]{3,2,1,0:T(8,128)S(1)}, f32[2,2,256,256]{3,2,1,0:T(8,128)S(1)}, u32[]{:S(2)}, u32[]{:S(2)}) %collective-permute-start.5) | collective-permute-done | bytes 1048608 | tf_op jit(solution)/shard_map/ppermute | solution.py:17
  (107 shorter events, 86.9 us)
Async XLA Ops:
  0.0 32.2 %copy-start.6 = (f32[2,31]{1,0:T(2,128)S(1)}, f32[2,31]{1,0:T(2,128)}, u32[]{:S(2)}) copy-start(f32[2,31]{1,0:T(2,128)} %param.20) | copy-start | bytes 748
  0.0 74.6 %copy-start.7 = (s32[1,2,2]{2,1,0:T(2,128)S(1)}, s32[1,2,2]{2,1,0:T(2,128)}, u32[]{:S(2)}) copy-start(s32[1,2,2]{2,1,0:T(2,128)} %param.22) | copy-start | bytes 52
  0.0 78.7 %copy-start.5 = (f32[2,2,1,256,256]{4,3,2,1,0:T(8,128)S(1)}, f32[2,2,1,256,256]{4,3,2,1,0:T(8,128)}, u32[]{:S(2)}) copy-start(f32[2,2,1,256,256]{4,3,2,1,0:T(8,128)} %param.18) | copy-start | bytes 3145732
  0.0 27.1 %collective-permute-start.2 = (f32[2,2,256,256]{3,2,1,0:T(8,128)}, f32[2,2,256,256]{3,2,1,0:T(8,128)S(1)}, u32[]{:S(2)}, u32[]{:S(2)}) collective-permute-start(f32[2,2,256,256]{3,2,1,0:T(8,128)} %bitcast.450), channel_id=1, source_target_pairs={{1,0},{2,1},{3,2},{4,3},{5,4},{6,5},{7,6},{8,7},{9,8},{10,9},{11,1... | collective-permute-start | bytes 3145736 | tf_op jit(solution)/shard_map/ppermute | solution.py:17
  30.0 48.7 %collective-permute-start.3 = (f32[2,2,256,512]{3,2,1,0:T(8,128)}, f32[2,2,256,512]{3,2,1,0:T(8,128)}, u32[]{:S(2)}, u32[]{:S(2)}) collective-permute-start(f32[2,2,256,512]{3,2,1,0:T(8,128)} %pad_maximum_fusion.5), channel_id=1, source_target_pairs={{4,0},{5,1},{6,2},{7,3},{8,4},{9,5},{10,6},{11,7},{12,8},{13,9},{1... | collective-permute-start | bytes 6291464 | tf_op jit(solution)/shard_map/ppermute | solution.py:17
  84.4 9.3 %copy-start.3 = (f32[2,256,256]{2,1,0:T(8,128)S(1)}, f32[2,256,256]{2,1,0:T(8,128)}, u32[]{:S(2)}) copy-start(f32[2,256,256]{2,1,0:T(8,128)} %param.19) | copy-start | bytes 1572868
  121.5 3.8 %collective-permute-start = (f32[2,2,256,256]{3,2,0,1:T(8,128)}, f32[2,2,256,256]{3,2,0,1:T(8,128)S(1)}, u32[]{:S(2)}, u32[]{:S(2)}) collective-permute-start(f32[2,2,256,256]{3,2,0,1:T(8,128)} %get-tuple-element.1418), channel_id=1, source_target_pairs={{0,16},{1,17},{2,18},{3,19},{4,20},{5,21},{6,22},{7,23},{8,24},{9,... | collective-permute-start | bytes 3145736 | tf_op jit(solution)/shard_map/while/body/eval_jaxpr/ppermute | solution.py:17
  127.0 28.9 %collective-permute-start = (f32[2,2,256,256]{3,2,0,1:T(8,128)}, f32[2,2,256,256]{3,2,0,1:T(8,128)S(1)}, u32[]{:S(2)}, u32[]{:S(2)}) collective-permute-start(f32[2,2,256,256]{3,2,0,1:T(8,128)} %get-tuple-element.1418), channel_id=1, source_target_pairs={{0,16},{1,17},{2,18},{3,19},{4,20},{5,21},{6,22},{7,23},{8,24},{9,... | collective-permute-start | bytes 3145736 | tf_op jit(solution)/shard_map/while/body/eval_jaxpr/ppermute | solution.py:17
  178.9 38.7 %collective-permute-start.1 = (f32[2,2,256,256]{3,2,0,1:T(8,128)S(1)}, f32[2,2,256,256]{3,2,0,1:T(8,128)}, u32[]{:S(2)}, u32[]{:S(2)}) collective-permute-start(f32[2,2,256,256]{3,2,0,1:T(8,128)S(1)} %get-tuple-element.1433), channel_id=1, source_target_pairs={{16,0},{17,1},{18,2},{19,3},{20,4},{21,5},{22,6},{23,7},{24,8},{25... | collective-permute-start | bytes 3145736 | tf_op jit(solution)/shard_map/while/body/eval_jaxpr/ppermute | solution.py:17
  222.1 1.0 copy-start.2
  228.4 3.1 copy-start
  244.3 4.7 %collective-permute-start.1 = (f32[2,2,256,256]{3,2,0,1:T(8,128)S(1)}, f32[2,2,256,256]{3,2,0,1:T(8,128)}, u32[]{:S(2)}, u32[]{:S(2)}) collective-permute-start(f32[2,2,256,256]{3,2,0,1:T(8,128)S(1)} %get-tuple-element.1433), channel_id=1, source_target_pairs={{16,0},{17,1},{18,2},{19,3},{20,4},{21,5},{22,6},{23,7},{24,8},{25... | collective-permute-start | bytes 3145736 | tf_op jit(solution)/shard_map/while/body/eval_jaxpr/ppermute | solution.py:17
  250.4 2.5 copy-start.8
  289.1 51.5 %copy-start.1 = (f32[2,2,512,512]{3,2,1,0:T(8,128)S(1)}, f32[2,2,512,512]{3,2,1,0:T(8,128)}, u32[]{:S(2)}) copy-start(f32[2,2,512,512]{3,2,1,0:T(8,128)} %get-tuple-element.828) | copy-start | bytes 12582916
  291.1 49.6 %collective-permute-start.4 = (f32[2,2,256,512]{3,2,1,0:T(8,128)S(1)}, f32[2,2,256,512]{3,2,1,0:T(8,128)S(1)}, u32[]{:S(2)}, u32[]{:S(2)}) collective-permute-start(f32[2,2,256,512]{3,2,1,0:T(8,128)S(1)} %slice.366), channel_id=1, source_target_pairs={{0,4},{1,5},{2,6},{3,7},{4,8},{5,9},{6,10},{7,11},{8,12},{9,13},{1... | collective-permute-start | bytes 6291464 | tf_op jit(solution)/shard_map/ppermute | solution.py:17
  341.2 28.1 %collective-permute-start.5 = (f32[2,2,256,256]{3,2,1,0:T(8,128)S(1)}, f32[2,2,256,256]{3,2,1,0:T(8,128)S(1)}, u32[]{:S(2)}, u32[]{:S(2)}) collective-permute-start(f32[2,2,256,256]{3,2,1,0:T(8,128)S(1)} %slice.397), channel_id=1, source_target_pairs={{0,1},{1,2},{2,3},{3,4},{4,5},{5,6},{6,7},{7,8},{8,9},{9,10},{10,1... | collective-permute-start | bytes 3145736 | tf_op jit(solution)/shard_map/ppermute | solution.py:17
where the time goes:
time: 377 us; the launch traced here: 371 us
  waiting for transfers between devices  144 us (38%)
  other arithmetic  65.4 us (17%)
  local copies, waits for them, and re-layouts  51.5 us (14%)
  starting transfers between devices  43.1 us (11%)
  matrix products  35.3 us (9%)
  loops' own time  31.4 us (8%)
    ppermute x8, waiting for transfers between devices, shifted(): return lax.ppermute(shard, axis, pairs)  144 us
    ppermute x8, starting transfers between devices, shifted(): return lax.ppermute(shard, axis, pairs)  43.1 us
    dot_general x32, matrix products, product(): return jnp.matmul(first, second, precision=HIGHEST)  35.3 us
    dynamic_update_slice x2, local copies, waits for them, and re-layouts, deposit(): lax.dynamic_update_slice(field, current + grads_all[slot_index], start_tu...  22.8 us
    another operation x1, loops' own time, local(): lax.fori_loop(0, round_count, up_round, (zero_batch, grads_all))  21.5 us
    add x1, other arithmetic, band_tables(): band_real = band_real + jnp.where(on_band, fresnel_taps[0, tap_index], 0.0)  19.8 us
    add x1, other arithmetic, band_tables(): band_imag = band_imag + jnp.where(on_band, fresnel_taps[1, tap_index], 0.0)  19.8 us
    gather x6, local copies, waits for them, and re-layouts  9.32 us
  transfers between devices with their start and end apart: 8, of which 8 were waited for; matrix products, arithmetic and copies ran while one was open for 11% of the time, Pallas kernels for 0%

commit v1 on v0

v1 whole, which is shorter than its diff:
```python
import math

import jax
import jax.numpy as jnp
import numpy as np
from jax import lax
from jax.experimental import pallas as pl
from jax.experimental.pallas import tpu as pltpu
from jax.sharding import PartitionSpec as P

GX = 4
F32 = jnp.float32
BF16 = jnp.bfloat16


def shifted(block, axis, by):
    peers = lax.axis_size(axis)
    pairs = [(i, i + by) for i in range(peers) if 0 <= i + by < peers]
    return lax.ppermute(block, axis, pairs)


def swapped(block):
    return lax.ppermute(block, "depth", [(0, 1), (1, 0)])


def halves(value):
    high = value.astype(BF16)
    return high, (value - high.astype(F32)).astype(BF16)


def fourier_planes(side):
    index = np.arange(side)
    phase = (index[:, None] * index[None, :] % side) * (2.0 * math.pi / side)
    planes = np.stack([np.cos(phase), -np.sin(phase)]) / math.sqrt(side)
    return planes.astype(np.float32)


def put_left(table, real, imag, row, rows):
    side = real.shape[1]
    rh, rl = halves(real)
    ih, il = halves(imag)
    for at, (top, low) in enumerate(((rh, ih), (rh, ih), (rl, il), (-ih, rh), (-ih, rh), (-il, rl))):
        cols = slice(at * side, (at + 1) * side)
        table[pl.ds(row, rows), cols] = top
        table[pl.ds(row + side, rows), cols] = low


def put_right(table, real, imag, row, rows):
    side = real.shape[1]
    rh, rl = halves(real)
    ih, il = halves(imag)
    for at, (first, second) in enumerate(((rh, ih), (rl, il), (rh, ih), (-ih, rh), (-il, rl), (-ih, rh))):
        table[pl.ds(row + at * side, rows), 0:side] = first
        table[pl.ds(row + at * side, rows), side:] = second


def from_left(table, stack, real, imag):
    side = real.shape[0]
    rh, rl = halves(real)
    ih, il = halves(imag)
    for at, part in enumerate((rh, rl, rh, ih, il, ih)):
        stack[at * side:(at + 1) * side, :] = part
    both = jnp.dot(table[...], stack[...], preferred_element_type=F32)
    return both[:side], both[side:]


def from_right(table, line, real, imag):
    side = real.shape[0]
    rh, rl = halves(real)
    ih, il = halves(imag)
    for at, part in enumerate((rh, rh, rl, ih, ih, il)):
        line[:, at * side:(at + 1) * side] = part
    both = jnp.dot(line[...], table[...], preferred_element_type=F32)
    return both[:, :side], both[:, side:]


def wave_kernel(
    scalars, taps, mine, other, probe, measured, fourier, grad_mine, grad_other,
    left_f, left_b, right_f, right_b, four_l, four_r, saved, stack, line,
):
    side = probe.shape[-1]
    per = mine.shape[0]
    layers = 2 * per
    row_at, col_at, live, depth = scalars[0], scalars[1], scalars[2], scalars[3]
    tap_count = taps.shape[1]
    half = tap_count // 2
    rows = 16

    @pl.when(live == 0)
    def _():
        grad_mine[...] = jnp.zeros_like(grad_mine)
        grad_other[...] = jnp.zeros_like(grad_other)

    @pl.when(live != 0)
    def _():
        def tables(block, unused):
            row = pl.multiple_of(block * rows, rows)
            i = lax.broadcasted_iota(jnp.int32, (rows, side), 0) + row
            j = lax.broadcasted_iota(jnp.int32, (rows, side), 1)
            lag = j - i
            lag = jnp.where(lag > side // 2, lag - side, lag)
            lag = jnp.where(lag < -(side // 2), lag + side, lag)
            zero = jnp.zeros((rows, side), F32)
            fr, fi, br, bi = zero, zero, zero, zero
            for tap in range(tap_count):
                on = lag == tap - half
                back = tap_count - 1 - tap
                fr = jnp.where(on, taps[0, tap], fr)
                fi = jnp.where(on, taps[1, tap], fi)
                br = jnp.where(on, taps[0, back], br)
                bi = jnp.where(on, taps[1, back], bi)

            def inside(corner):
                ii = jnp.where(i < corner, i + side, i)
                jj = jnp.where(j < corner, j + side, j)
                return jj - ii == lag

            keep = inside(row_at)
            put_left(left_f, jnp.where(keep, fr, 0.0), jnp.where(keep, fi, 0.0), row, rows)
            put_left(left_b, jnp.where(keep, br, 0.0), jnp.where(keep, -bi, 0.0), row, rows)
            keep = inside(col_at)
            put_right(right_f, jnp.where(keep, br, 0.0), jnp.where(keep, bi, 0.0), row, rows)
            put_right(right_b, jnp.where(keep, fr, 0.0), jnp.where(keep, -fi, 0.0), row, rows)
            return unused

        lax.fori_loop(0, side // rows, tables, 0)
        put_left(four_l, fourier[0], fourier[1], 0, side)
        put_right(four_r, fourier[0], fourier[1], 0, side)

        def layer(k):
            here = depth == k // per
            return [jnp.where(here, mine[k % per, c], other[k % per, c]) for c in range(2)]

        for c in range(2):
            saved[0, c] = pltpu.roll(pltpu.roll(probe[c], row_at, 0), col_at, 1)
        for k in range(layers):
            wr, wi = saved[k, 0], saved[k, 1]
            o_r, o_i = layer(k)
            wr, wi = wr * o_r - wi * o_i, wr * o_i + wi * o_r
            wr, wi = from_left(left_f, stack, wr, wi)
            wr, wi = from_right(right_f, line, wr, wi)
            if k < layers - 1:
                saved[k + 1, 0] = wr
                saved[k + 1, 1] = wi
        wr, wi = from_left(four_l, stack, wr, wi)
        wr, wi = from_right(four_r, line, wr, wi)
        misfit = 2.0 * (wr * wr + wi * wi - measured[depth])
        put_left(four_l, fourier[0], -fourier[1], 0, side)
        put_right(four_r, fourier[0], -fourier[1], 0, side)
        gr, gi = misfit * wr, misfit * wi
        gr, gi = from_left(four_l, stack, gr, gi)
        gr, gi = from_right(four_r, line, gr, gi)
        for k in reversed(range(layers)):
            gr, gi = from_left(left_b, stack, gr, gi)
            gr, gi = from_right(right_b, line, gr, gi)
            wr, wi = saved[k, 0], saved[k, 1]
            pr, pi = wr * gr + wi * gi, wr * gi - wi * gr

            @pl.when(depth == k // per)
            def _():
                grad_mine[k % per, 0] = pr
                grad_mine[k % per, 1] = pi

            @pl.when(depth != k // per)
            def _():
                grad_other[k % per, 0] = pr
                grad_other[k % per, 1] = pi

            if k > 0:
                o_r, o_i = layer(k)
                gr, gi = o_r * gr + o_i * gi, o_r * gi - o_i * gr


def wave_call(scalars, taps, mine, other, probe, measured, fourier):
    side = probe.shape[-1]
    per = mine.shape[0]
    vmem = pl.BlockSpec(memory_space=pltpu.VMEM)
    smem = pl.BlockSpec(memory_space=pltpu.SMEM)
    out = jax.ShapeDtypeStruct(mine.shape, F32)
    tall = pltpu.VMEM((6 * side, 2 * side), BF16)
    wide = pltpu.VMEM((2 * side, 6 * side), BF16)
    return pl.pallas_call(
        wave_kernel,
        out_shape=(out, out),
        in_specs=[smem, smem] + [vmem] * 5,
        out_specs=(vmem, vmem),
        scratch_shapes=[
            wide, wide, tall, tall, wide, tall,
            pltpu.VMEM((2 * per, 2, side, side), F32),
            pltpu.VMEM((6 * side, side), BF16),
            pltpu.VMEM((side, 6 * side), BF16),
        ],
        compiler_params=pltpu.CompilerParams(vmem_limit_bytes=44 * 1024 * 1024),
        name="wave",
    )(scalars, taps, mine, other, probe, measured, fourier)


def local(transmission, illumination, fresnel_taps, intensity, offsets, counts):
    own = transmission[:, :, 0]
    side = own.shape[-1]
    corners = offsets[0]
    depth = lax.axis_index("depth")
    right = shifted(own, "tiles", -1)
    lower = shifted(own, "tiles", -GX)
    diag = shifted(own, "tiles", -GX - 1)
    i = lax.broadcasted_iota(jnp.int32, (side, side), 0)
    j = lax.broadcasted_iota(jnp.int32, (side, side), 1)

    def masks(slot):
        return i >= corners[slot, 0], j >= corners[slot, 1]

    def mosaic(slot):
        below, past = masks(slot)
        return jnp.where(below, jnp.where(past, own, right), jnp.where(past, lower, diag))

    mine = mosaic(depth)
    other = swapped(mosaic(1 - depth))
    live = (depth < counts[0]).astype(jnp.int32)
    scalars = jnp.stack([corners[depth, 0], corners[depth, 1], live, depth.astype(jnp.int32)])
    grad_mine, grad_other = wave_call(
        scalars, fresnel_taps, mine, other, illumination, intensity[0], jnp.asarray(fourier_planes(side))
    )
    grad_swap = swapped(grad_other)
    first, second = masks(depth), masks(1 - depth)

    def part(down, across):
        def one(mask, grad):
            keep = (mask[0] if down else ~mask[0]) & (mask[1] if across else ~mask[1])
            return jnp.where(keep, grad, 0.0)

        return one(first, grad_mine) + one(second, grad_swap)

    from_diag = shifted(part(False, False), "tiles", GX + 1)
    from_lower = shifted(part(False, True), "tiles", GX)
    from_right = shifted(part(True, False), "tiles", 1)
    total = part(True, True) + from_right + from_lower + from_diag
    return total[:, :, None]


def solution(mesh):
    placed = (
        P("depth", None, "tiles", None, None),
        P(),
        P(),
        P("tiles", None, None, None),
        P("tiles", None, None),
        P("tiles"),
    )
    return jax.shard_map(
        local,
        mesh=mesh,
        in_specs=placed,
        out_specs=P("depth", None, "tiles", None, None),
        check_vma=False,
    )
```

time: 377 us -> 223 us (0.59)
  the two profiles are of different devices: /device:TPU:8 before, /device:TPU:22 now
where the time goes in v1:
time: 223 us; the launch traced here: 221 us
  waiting for transfers between devices  172 us (77%)
  starting transfers between devices  32.7 us (15%)
  other arithmetic  11.8 us (5%)
  local copies, waits for them, and re-layouts  4.04 us (2%)
    ppermute x6, waiting for transfers between devices, shifted(): return lax.ppermute(block, axis, pairs)  171 us
    ppermute x6, starting transfers between devices, shifted(): return lax.ppermute(block, axis, pairs)  32.5 us
  transfers between devices with their start and end apart: 8, of which 7 were waited for; matrix products, arithmetic and copies ran while one was open for 3% of the time, Pallas kernels for 0%

profile of v1, /device:TPU:22, one launch (start us, length us, event | category | flops | bytes accessed | tf_op | source)
XLA Modules:
  0.0 221.5 jit_solution(12612319431109889867)
XLA Ops:
  0.0 2.3 %collective-permute-start.1 = (f32[2,2,256,256]{3,2,1,0:T(8,128)}, f32[2,2,256,256]{3,2,1,0:T(8,128)S(1)}, u32[]{:S(2)}, u32[]{:S(2)}) collective-permute-start(f32[2,2,256,256]{3,2,1,0:T(8,128)} %bitcast.19), channel_id=1, source_target_pairs={{4,0},{5,1},{6,2},{7,3},{8,4},{9,5},{10,6},{11,7},{12,8},{13,9},{1... | collective-permute-start | bytes 3145736 | tf_op jit(solution)/shard_map/ppermute | solution.py:19
  2.4 2.4 %collective-permute-start.2 = (f32[2,2,256,256]{3,2,1,0:T(8,128)}, f32[2,2,256,256]{3,2,1,0:T(8,128)S(1)}, u32[]{:S(2)}, u32[]{:S(2)}) collective-permute-start(f32[2,2,256,256]{3,2,1,0:T(8,128)} %bitcast.20), channel_id=1, source_target_pairs={{5,0},{6,1},{7,2},{8,3},{9,4},{10,5},{11,6},{12,7},{13,8},{14,9},{... | collective-permute-start | bytes 3145736 | tf_op jit(solution)/shard_map/ppermute | solution.py:19
  4.8 3.3 %collective-permute-start = (f32[2,2,256,256]{3,2,1,0:T(8,128)}, f32[2,2,256,256]{3,2,1,0:T(8,128)S(1)}, u32[]{:S(2)}, u32[]{:S(2)}) collective-permute-start(f32[2,2,256,256]{3,2,1,0:T(8,128)} %bitcast.21), channel_id=1, source_target_pairs={{1,0},{2,1},{3,2},{4,3},{5,4},{6,5},{7,6},{8,7},{9,8},{10,9},{11,1... | collective-permute-start | bytes 3145736 | tf_op jit(solution)/shard_map/ppermute | solution.py:19
  9.4 1.3 iota_compare_fusion
  10.7 1.2 iota_compare_fusion.2
  11.9 16.2 %collective-permute-done.1 = f32[2,2,256,256]{3,2,1,0:T(8,128)S(1)} collective-permute-done((f32[2,2,256,256]{3,2,1,0:T(8,128)}, f32[2,2,256,256]{3,2,1,0:T(8,128)S(1)}, u32[]{:S(2)}, u32[]{:S(2)}) %collective-permute-start.1) | collective-permute-done | bytes 1048608 | tf_op jit(solution)/shard_map/ppermute | solution.py:19
  28.1 19.4 %collective-permute-done.2 = f32[2,2,256,256]{3,2,1,0:T(8,128)S(1)} collective-permute-done((f32[2,2,256,256]{3,2,1,0:T(8,128)}, f32[2,2,256,256]{3,2,1,0:T(8,128)S(1)}, u32[]{:S(2)}, u32[]{:S(2)}) %collective-permute-start.2) | collective-permute-done | bytes 1048608 | tf_op jit(solution)/shard_map/ppermute | solution.py:19
  47.6 24.3 %collective-permute-done = f32[2,2,256,256]{3,2,1,0:T(8,128)S(1)} collective-permute-done((f32[2,2,256,256]{3,2,1,0:T(8,128)}, f32[2,2,256,256]{3,2,1,0:T(8,128)S(1)}, u32[]{:S(2)}, u32[]{:S(2)}) %collective-permute-start) | collective-permute-done | bytes 1048608 | tf_op jit(solution)/shard_map/ppermute | solution.py:19
  71.9 1.0 copy-done.5
  72.9 3.2 %select_select_fusion = (f32[2,2,256,256]{3,2,1,0:T(8,128)}, f32[2,2,256,256]{3,2,1,0:T(8,128)S(1)}) fusion(f32[2,2,256,256]{3,2,1,0:T(8,128)S(1)} %collective-permute-done.1, f32[2,2,256,256]{3,2,1,0:T(8,128)} %copy-done.4, f32[2,2,256,256]{3,2,1,0:T(8,128)} %copy-done.5, pred[256]{0:T(512)(128)(4,1)S(1)} %get-tuple-element.27, ...), kind=kLoop, calls=%fused_computation.4 | loop fusion | flops 1572864 | bytes 6292480 | tf_op jit(solution)/shard_map/jit(_where)/select_n | solution.py:214
  76.8 1.3 pad_add_fusion.scalars
  78.1 0.9 collective-permute-done.3.other
  79.0 0.7 copy-done.3
  79.7 1.0 copy-done.2
  80.7 0.7 wave.1
  81.6 1.3 fusion.2
  82.9 1.2 fusion
  85.1 21.3 %collective-permute-start.5 = (f32[2,2,256,256]{3,2,1,0:T(8,128)S(1)}, f32[2,2,256,256]{3,2,1,0:T(8,128)S(1)}, u32[]{:S(2)}, u32[]{:S(2)}) collective-permute-start(f32[2,2,256,256]{3,2,1,0:T(8,128)S(1)} %get-tuple-element.11), channel_id=1, source_target_pairs={{0,1},{1,2},{2,3},{3,4},{4,5},{5,6},{6,7},{7,8},{8,9},{9,10},{10,1... | collective-permute-start | bytes 3145736 | tf_op jit(solution)/shard_map/ppermute | solution.py:19
  106.3 1.3 collective-permute-start.7
  107.6 1.9 collective-permute-start.6
  109.5 20.2 %collective-permute-done.5 = f32[2,2,256,256]{3,2,1,0:T(8,128)S(1)} collective-permute-done((f32[2,2,256,256]{3,2,1,0:T(8,128)S(1)}, f32[2,2,256,256]{3,2,1,0:T(8,128)S(1)}, u32[]{:S(2)}, u32[]{:S(2)}) %collective-permute-start.5) | collective-permute-done | bytes 1048608 | tf_op jit(solution)/shard_map/ppermute | solution.py:19
  129.8 7.5 %collective-permute-done.7 = f32[2,2,256,256]{3,2,1,0:T(8,128)S(1)} collective-permute-done((f32[2,2,256,256]{3,2,1,0:T(8,128)S(1)}, f32[2,2,256,256]{3,2,1,0:T(8,128)S(1)}, u32[]{:S(2)}, u32[]{:S(2)}) %collective-permute-start.7) | collective-permute-done | bytes 1048608 | tf_op jit(solution)/shard_map/ppermute | solution.py:19
  137.3 82.9 %collective-permute-done.6 = f32[2,2,256,256]{3,2,1,0:T(8,128)S(1)} collective-permute-done((f32[2,2,256,256]{3,2,1,0:T(8,128)S(1)}, f32[2,2,256,256]{3,2,1,0:T(8,128)S(1)}, u32[]{:S(2)}, u32[]{:S(2)}) %collective-permute-start.6) | collective-permute-done | bytes 1048608 | tf_op jit(solution)/shard_map/ppermute | solution.py:19
  220.2 1.3 add_bitcast_fusion
  (18 shorter events, 2.4 us)
Async XLA Ops:
  0.0 28.1 %collective-permute-start.1 = (f32[2,2,256,256]{3,2,1,0:T(8,128)}, f32[2,2,256,256]{3,2,1,0:T(8,128)S(1)}, u32[]{:S(2)}, u32[]{:S(2)}) collective-permute-start(f32[2,2,256,256]{3,2,1,0:T(8,128)} %bitcast.19), channel_id=1, source_target_pairs={{4,0},{5,1},{6,2},{7,3},{8,4},{9,5},{10,6},{11,7},{12,8},{13,9},{1... | collective-permute-start | bytes 3145736 | tf_op jit(solution)/shard_map/ppermute | solution.py:19
  2.4 45.2 %collective-permute-start.2 = (f32[2,2,256,256]{3,2,1,0:T(8,128)}, f32[2,2,256,256]{3,2,1,0:T(8,128)S(1)}, u32[]{:S(2)}, u32[]{:S(2)}) collective-permute-start(f32[2,2,256,256]{3,2,1,0:T(8,128)} %bitcast.20), channel_id=1, source_target_pairs={{5,0},{6,1},{7,2},{8,3},{9,4},{10,5},{11,6},{12,7},{13,8},{14,9},{... | collective-permute-start | bytes 3145736 | tf_op jit(solution)/shard_map/ppermute | solution.py:19
  4.8 67.1 %collective-permute-start = (f32[2,2,256,256]{3,2,1,0:T(8,128)}, f32[2,2,256,256]{3,2,1,0:T(8,128)S(1)}, u32[]{:S(2)}, u32[]{:S(2)}) collective-permute-start(f32[2,2,256,256]{3,2,1,0:T(8,128)} %bitcast.21), channel_id=1, source_target_pairs={{1,0},{2,1},{3,2},{4,3},{5,4},{6,5},{7,6},{8,7},{9,8},{10,9},{11,1... | collective-permute-start | bytes 3145736 | tf_op jit(solution)/shard_map/ppermute | solution.py:19
  8.1 0.7 copy-start.6
  47.6 24.3 %copy-start.4 = (f32[2,2,256,256]{3,2,1,0:T(8,128)}, f32[2,2,256,256]{3,2,1,0:T(8,128)S(1)}, u32[]{:S(2)}) copy-start(f32[2,2,256,256]{3,2,1,0:T(8,128)S(1)} %collective-permute-done.2) | copy-start | bytes 3145732
  71.9 1.0 copy-start.5
  72.9 6.1 %copy-start = (f32[2,256,256]{2,1,0:T(8,128)S(1)}, f32[2,256,256]{2,1,0:T(8,128)}, u32[]{:S(2)}) copy-start(f32[2,256,256]{2,1,0:T(8,128)} %probe.1) | copy-start | bytes 1572868
  72.9 6.1 %copy-start.1 = (f32[1,2,256,256]{3,2,1,0:T(8,128)S(1)}, f32[1,2,256,256]{3,2,1,0:T(8,128)}, u32[]{:S(2)}) copy-start(f32[1,2,256,256]{3,2,1,0:T(8,128)} %param.10) | copy-start | bytes 1572868
  76.1 2.9 %collective-permute-start.3 = (f32[2,2,256,256]{3,2,1,0:T(8,128)}, f32[2,2,256,256]{3,2,1,0:T(8,128)S(1)}, u32[]{:S(2)}, u32[]{:S(2)}) collective-permute-start(f32[2,2,256,256]{3,2,1,0:T(8,128)} %get-tuple-element.9), channel_id=1, source_target_pairs={{0,16},{16,0},{1,17},{17,1},{2,18},{18,2},{3,19},{19,3},{4,20},{20... | collective-permute-start | bytes 3145736 | tf_op jit(solution)/shard_map/ppermute | solution.py:23
  79.0 0.7 copy-start.3
  79.7 1.0 copy-start.2
  81.4 3.1 %collective-permute-start.4 = (f32[2,2,256,256]{3,2,1,0:T(8,128)S(1)}, f32[2,2,256,256]{3,2,1,0:T(8,128)S(1)}, u32[]{:S(2)}, u32[]{:S(2)}) collective-permute-start(f32[2,2,256,256]{3,2,1,0:T(8,128)S(1)} %get-tuple-element.8), channel_id=1, source_target_pairs={{0,16},{16,0},{1,17},{17,1},{2,18},{18,2},{3,19},{19,3},{4,20},{20... | collective-permute-start | bytes 3145736 | tf_op jit(solution)/shard_map/ppermute | solution.py:23
  85.1 44.7 %collective-permute-start.5 = (f32[2,2,256,256]{3,2,1,0:T(8,128)S(1)}, f32[2,2,256,256]{3,2,1,0:T(8,128)S(1)}, u32[]{:S(2)}, u32[]{:S(2)}) collective-permute-start(f32[2,2,256,256]{3,2,1,0:T(8,128)S(1)} %get-tuple-element.11), channel_id=1, source_target_pairs={{0,1},{1,2},{2,3},{3,4},{4,5},{5,6},{6,7},{7,8},{8,9},{9,10},{10,1... | collective-permute-start | bytes 3145736 | tf_op jit(solution)/shard_map/ppermute | solution.py:19
  106.3 31.0 %collective-permute-start.7 = (f32[2,2,256,256]{3,2,1,0:T(8,128)S(1)}, f32[2,2,256,256]{3,2,1,0:T(8,128)S(1)}, u32[]{:S(2)}, u32[]{:S(2)}) collective-permute-start(f32[2,2,256,256]{3,2,1,0:T(8,128)S(1)} %get-tuple-element.12), channel_id=1, source_target_pairs={{0,5},{1,6},{2,7},{3,8},{4,9},{5,10},{6,11},{7,12},{8,13},{9,14},{... | collective-permute-start | bytes 3145736 | tf_op jit(solution)/shard_map/ppermute | solution.py:19
  107.6 112.5 %collective-permute-start.6 = (f32[2,2,256,256]{3,2,1,0:T(8,128)S(1)}, f32[2,2,256,256]{3,2,1,0:T(8,128)S(1)}, u32[]{:S(2)}, u32[]{:S(2)}) collective-permute-start(f32[2,2,256,256]{3,2,1,0:T(8,128)S(1)} %get-tuple-element.13), channel_id=1, source_target_pairs={{0,4},{1,5},{2,6},{3,7},{4,8},{5,9},{6,10},{7,11},{8,12},{9,13},{1... | collective-permute-start | bytes 3145736 | tf_op jit(solution)/shard_map/ppermute | solution.py:19

commit v2 on v1

--- a/solution.py
+++ b/solution.py
@@ -13,10 +13,14 @@
 BF16 = jnp.bfloat16
 
 
-def shifted(block, axis, by):
-    peers = lax.axis_size(axis)
-    pairs = [(i, i + by) for i in range(peers) if 0 <= i + by < peers]
-    return lax.ppermute(block, axis, pairs)
+def shifted(block, rows, cols):
+    peers = lax.axis_size("tiles")
+    pairs = [
+        (i, i + rows * GX + cols)
+        for i in range(peers)
+        if 0 <= i // GX + rows < peers // GX and 0 <= i % GX + cols < GX
+    ]
+    return lax.ppermute(block, "tiles", pairs)
 
 
 def swapped(block):
@@ -200,9 +204,9 @@
     side = own.shape[-1]
     corners = offsets[0]
     depth = lax.axis_index("depth")
-    right = shifted(own, "tiles", -1)
-    lower = shifted(own, "tiles", -GX)
-    diag = shifted(own, "tiles", -GX - 1)
+    right = shifted(own, 0, -1)
+    lower = shifted(own, -1, 0)
+    diag = shifted(own, -1, -1)
     i = lax.broadcasted_iota(jnp.int32, (side, side), 0)
     j = lax.broadcasted_iota(jnp.int32, (side, side), 1)
 
@@ -230,9 +234,9 @@
 
         return one(first, grad_mine) + one(second, grad_swap)
 
-    from_diag = shifted(part(False, False), "tiles", GX + 1)
-    from_lower = shifted(part(False, True), "tiles", GX)
-    from_right = shifted(part(True, False), "tiles", 1)
+    from_diag = shifted(part(False, False), 1, 1)
+    from_lower = shifted(part(False, True), 1, 0)
+    from_right = shifted(part(True, False), 0, 1)
     total = part(True, True) + from_right + from_lower + from_diag
     return total[:, :, None]
 

time: 223 us -> 143 us (0.64)
  the two profiles are of different devices: /device:TPU:22 before, /device:TPU:8 now
where the time goes in v2:
time: 143 us; the launch traced here: 142 us
  waiting for transfers between devices  90.8 us (63%)
  Pallas kernels  20.5 us (14%)
  starting transfers between devices  14 us (10%)
  other arithmetic  11.8 us (8%)
  local copies, waits for them, and re-layouts  4.04 us (3%)
    ppermute x6, waiting for transfers between devices, shifted(): return lax.ppermute(block, 'tiles', pairs)  89.9 us
    pallas_call x1, Pallas kernels, wave_call(): pl.pallas_call(wave_kernel, out_shape=(out, out), in_specs=[smem, smem] +...  20.5 us
    ppermute x6, starting transfers between devices, shifted(): return lax.ppermute(block, 'tiles', pairs)  14 us
    unnamed x14, local copies, waits for them, and re-layouts  3.39 us
    select_n x1, other arithmetic, mosaic(): jnp.where(below, jnp.where(past, own, right), jnp.where(past, lower, diag))  3.24 us
  transfers between devices with their start and end apart: 8, of which 6 were waited for; matrix products, arithmetic and copies ran while one was open for 5% of the time, Pallas kernels for 0%

profile of v2, /device:TPU:8, one launch (start us, length us, event | category | flops | bytes accessed | tf_op | source)
XLA Modules:
  0.0 141.9 jit_solution(11425810280764802678)
XLA Ops:
  0.0 1.9 %collective-permute-start.1 = (f32[2,2,256,256]{3,2,1,0:T(8,128)}, f32[2,2,256,256]{3,2,1,0:T(8,128)S(1)}, u32[]{:S(2)}, u32[]{:S(2)}) collective-permute-start(f32[2,2,256,256]{3,2,1,0:T(8,128)} %bitcast.19), channel_id=1, source_target_pairs={{4,0},{5,1},{6,2},{7,3},{8,4},{9,5},{10,6},{11,7},{12,8},{13,9},{1... | collective-permute-start | bytes 3145736 | tf_op jit(solution)/shard_map/ppermute | solution.py:23
  1.9 1.3 collective-permute-start.2
  3.2 1.3 collective-permute-start
  4.5 0.7 copy-done.6
  5.9 1.3 iota_compare_fusion
  7.1 1.2 iota_compare_fusion.2
  8.4 18.6 %collective-permute-done.1 = f32[2,2,256,256]{3,2,1,0:T(8,128)S(1)} collective-permute-done((f32[2,2,256,256]{3,2,1,0:T(8,128)}, f32[2,2,256,256]{3,2,1,0:T(8,128)S(1)}, u32[]{:S(2)}, u32[]{:S(2)}) %collective-permute-start.1) | collective-permute-done | bytes 1048608 | tf_op jit(solution)/shard_map/ppermute | solution.py:23
  27.0 23.5 %collective-permute-done.2 = f32[2,2,256,256]{3,2,1,0:T(8,128)S(1)} collective-permute-done((f32[2,2,256,256]{3,2,1,0:T(8,128)}, f32[2,2,256,256]{3,2,1,0:T(8,128)S(1)}, u32[]{:S(2)}, u32[]{:S(2)}) %collective-permute-start.2) | collective-permute-done | bytes 1048608 | tf_op jit(solution)/shard_map/ppermute | solution.py:23
  50.5 2.7 %collective-permute-done = f32[2,2,256,256]{3,2,1,0:T(8,128)S(1)} collective-permute-done((f32[2,2,256,256]{3,2,1,0:T(8,128)}, f32[2,2,256,256]{3,2,1,0:T(8,128)S(1)}, u32[]{:S(2)}, u32[]{:S(2)}) %collective-permute-start) | collective-permute-done | bytes 1048608 | tf_op jit(solution)/shard_map/ppermute | solution.py:23
  53.2 1.0 copy-done.5
  54.2 3.2 %select_select_fusion = (f32[2,2,256,256]{3,2,1,0:T(8,128)}, f32[2,2,256,256]{3,2,1,0:T(8,128)S(1)}) fusion(f32[2,2,256,256]{3,2,1,0:T(8,128)S(1)} %collective-permute-done.1, f32[2,2,256,256]{3,2,1,0:T(8,128)} %copy-done.4, f32[2,2,256,256]{3,2,1,0:T(8,128)} %copy-done.5, pred[256]{0:T(512)(128)(4,1)S(1)} %get-tuple-element.27, ...), kind=kLoop, calls=%fused_computation.4 | loop fusion | flops 1572864 | bytes 6292480 | tf_op jit(solution)/shard_map/jit(_where)/select_n | solution.py:218
  58.1 1.3 pad_add_fusion.scalars
  59.5 0.9 collective-permute-done.3.other
  60.4 0.7 copy-done.3
  61.0 1.0 copy-done.2
  62.1 20.5 %wave.1 = (f32[2,2,256,256]{3,2,1,0:T(8,128)S(1)}, f32[2,2,256,256]{3,2,1,0:T(8,128)S(1)}) custom-call(s32[4]{0:T(128)S(1)} %pad_add_fusion.scalars, f32[2,31]{1,0:T(2,128)S(1)} %copy-done.3, f32[2,2,256,256]{3,2,1,0:T(8,128)S(1)} %get-tuple-element.10.mine, f32[2,2,256,256]{3,2,1,0:T(8,128)S(1)} %collective-permute-done.3.other, ...), custom_call_target="tpu_custom_call" | custom-call | tf_op jit(solution)/shard_map/wave/pallas_call | solution.py:186
  82.7 1.3 fusion.2
  83.9 1.2 fusion
  86.1 4.6 %collective-permute-start.5 = (f32[2,2,256,256]{3,2,1,0:T(8,128)S(1)}, f32[2,2,256,256]{3,2,1,0:T(8,128)S(1)}, u32[]{:S(2)}, u32[]{:S(2)}) collective-permute-start(f32[2,2,256,256]{3,2,1,0:T(8,128)S(1)} %get-tuple-element.11), channel_id=1, source_target_pairs={{0,1},{1,2},{2,3},{4,5},{5,6},{6,7},{8,9},{9,10},{10,11},{12,13},{... | collective-permute-start | bytes 3145736 | tf_op jit(solution)/shard_map/ppermute | solution.py:23
  90.7 2.9 %collective-permute-start.7 = (f32[2,2,256,256]{3,2,1,0:T(8,128)S(1)}, f32[2,2,256,256]{3,2,1,0:T(8,128)S(1)}, u32[]{:S(2)}, u32[]{:S(2)}) collective-permute-start(f32[2,2,256,256]{3,2,1,0:T(8,128)S(1)} %get-tuple-element.12), channel_id=1, source_target_pairs={{0,5},{1,6},{2,7},{4,9},{5,10},{6,11},{8,13},{9,14},{10,15},{16,21... | collective-permute-start | bytes 3145736 | tf_op jit(solution)/shard_map/ppermute | solution.py:23
  93.6 1.9 %collective-permute-start.6 = (f32[2,2,256,256]{3,2,1,0:T(8,128)S(1)}, f32[2,2,256,256]{3,2,1,0:T(8,128)S(1)}, u32[]{:S(2)}, u32[]{:S(2)}) collective-permute-start(f32[2,2,256,256]{3,2,1,0:T(8,128)S(1)} %get-tuple-element.13), channel_id=1, source_target_pairs={{0,4},{1,5},{2,6},{3,7},{4,8},{5,9},{6,10},{7,11},{8,12},{9,13},{1... | collective-permute-start | bytes 3145736 | tf_op jit(solution)/shard_map/ppermute | solution.py:23
  95.6 40.6 %collective-permute-done.5 = f32[2,2,256,256]{3,2,1,0:T(8,128)S(1)} collective-permute-done((f32[2,2,256,256]{3,2,1,0:T(8,128)S(1)}, f32[2,2,256,256]{3,2,1,0:T(8,128)S(1)}, u32[]{:S(2)}, u32[]{:S(2)}) %collective-permute-start.5) | collective-permute-done | bytes 1048608 | tf_op jit(solution)/shard_map/ppermute | solution.py:23
  136.2 4.4 %collective-permute-done.6 = f32[2,2,256,256]{3,2,1,0:T(8,128)S(1)} collective-permute-done((f32[2,2,256,256]{3,2,1,0:T(8,128)S(1)}, f32[2,2,256,256]{3,2,1,0:T(8,128)S(1)}, u32[]{:S(2)}, u32[]{:S(2)}) %collective-permute-start.6) | collective-permute-done | bytes 1048608 | tf_op jit(solution)/shard_map/ppermute | solution.py:23
  140.6 1.3 add_bitcast_fusion
  (18 shorter events, 1.6 us)
Async XLA Ops:
  0.0 27.0 %collective-permute-start.1 = (f32[2,2,256,256]{3,2,1,0:T(8,128)}, f32[2,2,256,256]{3,2,1,0:T(8,128)S(1)}, u32[]{:S(2)}, u32[]{:S(2)}) collective-permute-start(f32[2,2,256,256]{3,2,1,0:T(8,128)} %bitcast.19), channel_id=1, source_target_pairs={{4,0},{5,1},{6,2},{7,3},{8,4},{9,5},{10,6},{11,7},{12,8},{13,9},{1... | collective-permute-start | bytes 3145736 | tf_op jit(solution)/shard_map/ppermute | solution.py:23
  1.9 48.6 %collective-permute-start.2 = (f32[2,2,256,256]{3,2,1,0:T(8,128)}, f32[2,2,256,256]{3,2,1,0:T(8,128)S(1)}, u32[]{:S(2)}, u32[]{:S(2)}) collective-permute-start(f32[2,2,256,256]{3,2,1,0:T(8,128)} %bitcast.20), channel_id=1, source_target_pairs={{5,0},{6,1},{7,2},{9,4},{10,5},{11,6},{13,8},{14,9},{15,10},{21,16... | collective-permute-start | bytes 3145736 | tf_op jit(solution)/shard_map/ppermute | solution.py:23
  3.2 50.0 %collective-permute-start = (f32[2,2,256,256]{3,2,1,0:T(8,128)}, f32[2,2,256,256]{3,2,1,0:T(8,128)S(1)}, u32[]{:S(2)}, u32[]{:S(2)}) collective-permute-start(f32[2,2,256,256]{3,2,1,0:T(8,128)} %bitcast.21), channel_id=1, source_target_pairs={{1,0},{2,1},{3,2},{5,4},{6,5},{7,6},{9,8},{10,9},{11,10},{13,12},{... | collective-permute-start | bytes 3145736 | tf_op jit(solution)/shard_map/ppermute | solution.py:23
  4.5 0.7 copy-start.6
  50.5 2.7 %copy-start.4 = (f32[2,2,256,256]{3,2,1,0:T(8,128)}, f32[2,2,256,256]{3,2,1,0:T(8,128)S(1)}, u32[]{:S(2)}) copy-start(f32[2,2,256,256]{3,2,1,0:T(8,128)S(1)} %collective-permute-done.2) | copy-start | bytes 3145732
  53.2 1.0 copy-start.5
  54.2 6.1 %copy-start = (f32[2,256,256]{2,1,0:T(8,128)S(1)}, f32[2,256,256]{2,1,0:T(8,128)}, u32[]{:S(2)}) copy-start(f32[2,256,256]{2,1,0:T(8,128)} %probe.1) | copy-start | bytes 1572868
  54.2 6.1 %copy-start.1 = (f32[1,2,256,256]{3,2,1,0:T(8,128)S(1)}, f32[1,2,256,256]{3,2,1,0:T(8,128)}, u32[]{:S(2)}) copy-start(f32[1,2,256,256]{3,2,1,0:T(8,128)} %param.10) | copy-start | bytes 1572868
  57.5 2.9 %collective-permute-start.3 = (f32[2,2,256,256]{3,2,1,0:T(8,128)}, f32[2,2,256,256]{3,2,1,0:T(8,128)S(1)}, u32[]{:S(2)}, u32[]{:S(2)}) collective-permute-start(f32[2,2,256,256]{3,2,1,0:T(8,128)} %get-tuple-element.9), channel_id=1, source_target_pairs={{0,16},{16,0},{1,17},{17,1},{2,18},{18,2},{3,19},{19,3},{4,20},{20... | collective-permute-start | bytes 3145736 | tf_op jit(solution)/shard_map/ppermute | solution.py:27
  60.3 0.7 copy-start.3
  61.0 1.0 copy-start.2
  82.6 3.0 %collective-permute-start.4 = (f32[2,2,256,256]{3,2,1,0:T(8,128)S(1)}, f32[2,2,256,256]{3,2,1,0:T(8,128)S(1)}, u32[]{:S(2)}, u32[]{:S(2)}) collective-permute-start(f32[2,2,256,256]{3,2,1,0:T(8,128)S(1)} %get-tuple-element.8), channel_id=1, source_target_pairs={{0,16},{16,0},{1,17},{17,1},{2,18},{18,2},{3,19},{19,3},{4,20},{20... | collective-permute-start | bytes 3145736 | tf_op jit(solution)/shard_map/ppermute | solution.py:27
  86.1 50.1 %collective-permute-start.5 = (f32[2,2,256,256]{3,2,1,0:T(8,128)S(1)}, f32[2,2,256,256]{3,2,1,0:T(8,128)S(1)}, u32[]{:S(2)}, u32[]{:S(2)}) collective-permute-start(f32[2,2,256,256]{3,2,1,0:T(8,128)S(1)} %get-tuple-element.11), channel_id=1, source_target_pairs={{0,1},{1,2},{2,3},{4,5},{5,6},{6,7},{8,9},{9,10},{10,11},{12,13},{... | collective-permute-start | bytes 3145736 | tf_op jit(solution)/shard_map/ppermute | solution.py:23
  90.7 45.5 %collective-permute-start.7 = (f32[2,2,256,256]{3,2,1,0:T(8,128)S(1)}, f32[2,2,256,256]{3,2,1,0:T(8,128)S(1)}, u32[]{:S(2)}, u32[]{:S(2)}) collective-permute-start(f32[2,2,256,256]{3,2,1,0:T(8,128)S(1)} %get-tuple-element.12), channel_id=1, source_target_pairs={{0,5},{1,6},{2,7},{4,9},{5,10},{6,11},{8,13},{9,14},{10,15},{16,21... | collective-permute-start | bytes 3145736 | tf_op jit(solution)/shard_map/ppermute | solution.py:23
  93.6 47.0 %collective-permute-start.6 = (f32[2,2,256,256]{3,2,1,0:T(8,128)S(1)}, f32[2,2,256,256]{3,2,1,0:T(8,128)S(1)}, u32[]{:S(2)}, u32[]{:S(2)}) collective-permute-start(f32[2,2,256,256]{3,2,1,0:T(8,128)S(1)} %get-tuple-element.13), channel_id=1, source_target_pairs={{0,4},{1,5},{2,6},{3,7},{4,8},{5,9},{6,10},{7,11},{8,12},{9,13},{1... | collective-permute-start | bytes 3145736 | tf_op jit(solution)/shard_map/ppermute | solution.py:23

commit v3 on v2

--- a/solution.py
+++ b/solution.py
@@ -78,17 +78,74 @@
     return both[:, :side], both[:, side:]
 
 
-def wave_kernel(
-    scalars, taps, mine, other, probe, measured, fourier, grad_mine, grad_other,
-    left_f, left_b, right_f, right_b, four_l, four_r, saved, stack, line,
+def table_kernel(
+    scalars, taps, probe, fourier,
+    left_f, left_b, right_f, right_b, far_lf, far_lb, far_rf, far_rb, rolled,
+    four_l, four_r, band, stack, line,
 ):
     side = probe.shape[-1]
-    per = mine.shape[0]
-    layers = 2 * per
-    row_at, col_at, live, depth = scalars[0], scalars[1], scalars[2], scalars[3]
+    row_at, col_at = scalars[0], scalars[1]
     tap_count = taps.shape[1]
     half = tap_count // 2
     rows = 16
+    for c in range(2):
+        rolled[c] = pltpu.roll(pltpu.roll(probe[c], row_at, 0), col_at, 1)
+
+    def tables(block, unused):
+        row = pl.multiple_of(block * rows, rows)
+        i = lax.broadcasted_iota(jnp.int32, (rows, side), 0) + row
+        j = lax.broadcasted_iota(jnp.int32, (rows, side), 1)
+        lag = j - i
+        lag = jnp.where(lag > side // 2, lag - side, lag)
+        lag = jnp.where(lag < -(side // 2), lag + side, lag)
+        zero = jnp.zeros((rows, side), F32)
+        fr, fi, br, bi = zero, zero, zero, zero
+        for tap in range(tap_count):
+            on = lag == tap - half
+            back = tap_count - 1 - tap
+            fr = jnp.where(on, taps[0, tap], fr)
+            fi = jnp.where(on, taps[1, tap], fi)
+            br = jnp.where(on, taps[0, back], br)
+            bi = jnp.where(on, taps[1, back], bi)
+
+        def inside(corner):
+            ii = jnp.where(i < corner, i + side, i)
+            jj = jnp.where(j < corner, j + side, j)
+            return jj - ii == lag
+
+        keep = inside(row_at)
+        real, imag = jnp.where(keep, fr, 0.0), jnp.where(keep, fi, 0.0)
+        band[0, pl.ds(row, rows), :] = real
+        band[1, pl.ds(row, rows), :] = imag
+        put_left(left_f, real, imag, row, rows)
+        put_left(left_b, jnp.where(keep, br, 0.0), jnp.where(keep, -bi, 0.0), row, rows)
+        keep = inside(col_at)
+        real, imag = jnp.where(keep, br, 0.0), jnp.where(keep, bi, 0.0)
+        band[2, pl.ds(row, rows), :] = real
+        band[3, pl.ds(row, rows), :] = imag
+        put_right(right_f, real, imag, row, rows)
+        put_right(right_b, jnp.where(keep, fr, 0.0), jnp.where(keep, -fi, 0.0), row, rows)
+        return unused
+
+    lax.fori_loop(0, side // rows, tables, 0)
+    put_left(four_l, fourier[0], fourier[1], 0, side)
+    put_right(four_r, fourier[0], fourier[1], 0, side)
+    real, imag = from_left(four_l, stack, band[0], band[1])
+    put_left(far_lf, real, imag, 0, side)
+    put_left(far_lb, real.T, -imag.T, 0, side)
+    real, imag = from_right(four_r, line, band[2], band[3])
+    put_right(far_rf, real, imag, 0, side)
+    put_right(far_rb, real.T, -imag.T, 0, side)
+
+
+def wave_kernel(
+    scalars, mine, other, probe, measured,
+    left_f, left_b, right_f, right_b, far_lf, far_lb, far_rf, far_rb,
+    grad_mine, grad_other, saved, stack, line,
+):
+    per = mine.shape[0]
+    layers = 2 * per
+    live, depth = scalars[2], scalars[3]
 
     @pl.when(live == 0)
     def _():
@@ -97,67 +154,28 @@
 
     @pl.when(live != 0)
     def _():
-        def tables(block, unused):
-            row = pl.multiple_of(block * rows, rows)
-            i = lax.broadcasted_iota(jnp.int32, (rows, side), 0) + row
-            j = lax.broadcasted_iota(jnp.int32, (rows, side), 1)
-            lag = j - i
-            lag = jnp.where(lag > side // 2, lag - side, lag)
-            lag = jnp.where(lag < -(side // 2), lag + side, lag)
-            zero = jnp.zeros((rows, side), F32)
-            fr, fi, br, bi = zero, zero, zero, zero
-            for tap in range(tap_count):
-                on = lag == tap - half
-                back = tap_count - 1 - tap
-                fr = jnp.where(on, taps[0, tap], fr)
-                fi = jnp.where(on, taps[1, tap], fi)
-                br = jnp.where(on, taps[0, back], br)
-                bi = jnp.where(on, taps[1, back], bi)
-
-            def inside(corner):
-                ii = jnp.where(i < corner, i + side, i)
-                jj = jnp.where(j < corner, j + side, j)
-                return jj - ii == lag
-
-            keep = inside(row_at)
-            put_left(left_f, jnp.where(keep, fr, 0.0), jnp.where(keep, fi, 0.0), row, rows)
-            put_left(left_b, jnp.where(keep, br, 0.0), jnp.where(keep, -bi, 0.0), row, rows)
-            keep = inside(col_at)
-            put_right(right_f, jnp.where(keep, br, 0.0), jnp.where(keep, bi, 0.0), row, rows)
-            put_right(right_b, jnp.where(keep, fr, 0.0), jnp.where(keep, -fi, 0.0), row, rows)
-            return unused
-
-        lax.fori_loop(0, side // rows, tables, 0)
-        put_left(four_l, fourier[0], fourier[1], 0, side)
-        put_right(four_r, fourier[0], fourier[1], 0, side)
-
         def layer(k):
             here = depth == k // per
             return [jnp.where(here, mine[k % per, c], other[k % per, c]) for c in range(2)]
 
-        for c in range(2):
-            saved[0, c] = pltpu.roll(pltpu.roll(probe[c], row_at, 0), col_at, 1)
+        wr, wi = probe[0], probe[1]
         for k in range(layers):
-            wr, wi = saved[k, 0], saved[k, 1]
+            last = k == layers - 1
             o_r, o_i = layer(k)
             wr, wi = wr * o_r - wi * o_i, wr * o_i + wi * o_r
-            wr, wi = from_left(left_f, stack, wr, wi)
-            wr, wi = from_right(right_f, line, wr, wi)
-            if k < layers - 1:
-                saved[k + 1, 0] = wr
-                saved[k + 1, 1] = wi
-        wr, wi = from_left(four_l, stack, wr, wi)
-        wr, wi = from_right(four_r, line, wr, wi)
+            wr, wi = from_left(far_lf if last else left_f, stack, wr, wi)
+            wr, wi = from_right(far_rf if last else right_f, line, wr, wi)
+            if not last:
+                saved[k, 0] = wr
+                saved[k, 1] = wi
         misfit = 2.0 * (wr * wr + wi * wi - measured[depth])
-        put_left(four_l, fourier[0], -fourier[1], 0, side)
-        put_right(four_r, fourier[0], -fourier[1], 0, side)
         gr, gi = misfit * wr, misfit * wi
-        gr, gi = from_left(four_l, stack, gr, gi)
-        gr, gi = from_right(four_r, line, gr, gi)
         for k in reversed(range(layers)):
-            gr, gi = from_left(left_b, stack, gr, gi)
-            gr, gi = from_right(right_b, line, gr, gi)
-            wr, wi = saved[k, 0], saved[k, 1]
+            last = k == layers - 1
+            gr, gi = from_left(far_lb if last else left_b, stack, gr, gi)
+            gr, gi = from_right(far_rb if last else right_b, line, gr, gi)
+            wave = saved.at[k - 1] if k > 0 else probe
+            wr, wi = wave[0], wave[1]
             pr, pi = wr * gr + wi * gi, wr * gi - wi * gr
 
             @pl.when(depth == k // per)
@@ -175,28 +193,49 @@
                 gr, gi = o_r * gr + o_i * gi, o_r * gi - o_i * gr
 
 
-def wave_call(scalars, taps, mine, other, probe, measured, fourier):
+def wave_tables(scalars, taps, probe, fourier):
+    side = probe.shape[-1]
+    vmem = pl.BlockSpec(memory_space=pltpu.VMEM)
+    smem = pl.BlockSpec(memory_space=pltpu.SMEM)
+    tall = jax.ShapeDtypeStruct((6 * side, 2 * side), BF16)
+    wide = jax.ShapeDtypeStruct((2 * side, 6 * side), BF16)
+    return pl.pallas_call(
+        table_kernel,
+        out_shape=(wide, wide, tall, tall, wide, wide, tall, tall, jax.ShapeDtypeStruct(probe.shape, F32)),
+        in_specs=[smem, smem, vmem, vmem],
+        out_specs=(vmem,) * 9,
+        scratch_shapes=[
+            pltpu.VMEM(wide.shape, BF16),
+            pltpu.VMEM(tall.shape, BF16),
+            pltpu.VMEM((4, side, side), F32),
+            pltpu.VMEM((6 * side, side), BF16),
+            pltpu.VMEM((side, 6 * side), BF16),
+        ],
+        cost_estimate=pl.CostEstimate(flops=10**10, bytes_accessed=30 * 10**6, transcendentals=0),
+        compiler_params=pltpu.CompilerParams(vmem_limit_bytes=36 * 1024 * 1024),
+        name="tables",
+    )(scalars, taps, probe, fourier)
+
+
+def wave_call(scalars, mine, other, probe, measured, tables):
     side = probe.shape[-1]
     per = mine.shape[0]
     vmem = pl.BlockSpec(memory_space=pltpu.VMEM)
     smem = pl.BlockSpec(memory_space=pltpu.SMEM)
     out = jax.ShapeDtypeStruct(mine.shape, F32)
-    tall = pltpu.VMEM((6 * side, 2 * side), BF16)
-    wide = pltpu.VMEM((2 * side, 6 * side), BF16)
     return pl.pallas_call(
         wave_kernel,
         out_shape=(out, out),
-        in_specs=[smem, smem] + [vmem] * 5,
+        in_specs=[smem] + [vmem] * 12,
         out_specs=(vmem, vmem),
         scratch_shapes=[
-            wide, wide, tall, tall, wide, tall,
-            pltpu.VMEM((2 * per, 2, side, side), F32),
+            pltpu.VMEM((2 * per - 1, 2, side, side), F32),
             pltpu.VMEM((6 * side, side), BF16),
             pltpu.VMEM((side, 6 * side), BF16),
         ],
-        compiler_params=pltpu.CompilerParams(vmem_limit_bytes=44 * 1024 * 1024),
+        compiler_params=pltpu.CompilerParams(vmem_limit_bytes=40 * 1024 * 1024),
         name="wave",
-    )(scalars, taps, mine, other, probe, measured, fourier)
+    )(scalars, mine, other, probe, measured, *tables)
 
 
 def local(transmission, illumination, fresnel_taps, intensity, offsets, counts):
@@ -217,13 +256,13 @@
         below, past = masks(slot)
         return jnp.where(below, jnp.where(past, own, right), jnp.where(past, lower, diag))
 
-    mine = mosaic(depth)
-    other = swapped(mosaic(1 - depth))
     live = (depth < counts[0]).astype(jnp.int32)
     scalars = jnp.stack([corners[depth, 0], corners[depth, 1], live, depth.astype(jnp.int32)])
-    grad_mine, grad_other = wave_call(
-        scalars, fresnel_taps, mine, other, illumination, intensity[0], jnp.asarray(fourier_planes(side))
-    )
+    *tables, probe = wave_tables(scalars, fresnel_taps, illumination, jnp.asarray(fourier_planes(side)))
+    right, lower, diag, probe, tables = lax.optimization_barrier((right, lower, diag, probe, tables))
+    other = swapped(mosaic(1 - depth))
+    mine = mosaic(depth)
+    grad_mine, grad_other = wave_call(scalars, mine, other, probe, intensity[0], tables)
     grad_swap = swapped(grad_other)
     first, second = masks(depth), masks(1 - depth)
 

time: 143 us -> 131 us (0.916)
  starting transfers between devices: 14 us -> 29.1 us
  Pallas kernels: 20.5 us -> 7.33 us
  waiting for transfers between devices: 90.8 us -> 80.7 us
  other arithmetic: 11.8 us -> 6.61 us
    ppermute x6, starting transfers between devices: 14 us -> 28.8 us  [shifted(): return lax.ppermute(block, 'tiles', pairs)]
    ppermute x6, waiting for transfers between devices: 89.9 us -> 75.9 us  [shifted(): return lax.ppermute(block, 'tiles', pairs)]
    pallas_call x1 -> x2, Pallas kernels: 20.5 us -> 7.33 us  [the longest x1 4.82 us: wave_tables(): pl.pallas_call(table_kernel, out_shape=(wide, wide, tall, tall, wide, wid...]
    ppermute x2, waiting for transfers between devices: 0.9 us -> 4.78 us  [swapped(): return lax.ppermute(block, 'depth', [(0, 1), (1, 0)])]
    select_n x1, other arithmetic: 3.24 us -> 0.37 us  [mosaic(): jnp.where(below, jnp.where(past, own, right), jnp.where(past, lower, diag))]
    not x2 -> x0, other arithmetic: 2.5 us -> none  [one(): keep = (mask[0] if down else ~mask[0]) & (mask[1] if across else ~mask[1])]
    unnamed x14 -> x16, local copies, waits for them, and re-layouts: 3.39 us -> 3.95 us
  transfers between devices with their start and end apart: 8 -> 8, of which waited for: 6 -> 8; matrix products, arithmetic and copies ran while one was open for 5% -> 5% of each run, Pallas kernels for 0% -> 4%
where the time goes in v3:
time: 131 us; the launch traced here: 130 us
  waiting for transfers between devices  80.7 us (62%)
  starting transfers between devices  29.1 us (22%)
  Pallas kernels  7.33 us (6%)
  other arithmetic  6.61 us (5%)
  local copies, waits for them, and re-layouts  5.45 us (4%)
    ppermute x6, waiting for transfers between devices, shifted(): return lax.ppermute(block, 'tiles', pairs)  75.9 us
    ppermute x6, starting transfers between devices, shifted(): return lax.ppermute(block, 'tiles', pairs)  28.8 us
    pallas_call x1, Pallas kernels, wave_tables(): pl.pallas_call(table_kernel, out_shape=(wide, wide, tall, tall, wide, wid...  4.82 us
    ppermute x2, waiting for transfers between devices, swapped(): return lax.ppermute(block, 'depth', [(0, 1), (1, 0)])  4.78 us
    unnamed x16, local copies, waits for them, and re-layouts  3.95 us
    ge x4, other arithmetic, masks(): return (i >= corners[slot, 0], j >= corners[slot, 1])  2.62 us
  transfers between devices with their start and end apart: 8, of which 8 were waited for; matrix products, arithmetic and copies ran while one was open for 5% of the time, Pallas kernels for 4%

profile of v3, /device:TPU:8, one launch (start us, length us, event | category | flops | bytes accessed | tf_op | source)
XLA Modules:
  0.0 130.0 jit_solution(6608265251694699891)
XLA Ops:
  0.0 1.3 collective-permute-start
  1.3 1.9 %collective-permute-start.1 = (f32[2,2,256,256]{3,2,1,0:T(8,128)}, f32[2,2,256,256]{3,2,1,0:T(8,128)S(1)}, u32[]{:S(2)}, u32[]{:S(2)}) collective-permute-start(f32[2,2,256,256]{3,2,1,0:T(8,128)} %bitcast.20), channel_id=1, source_target_pairs={{4,0},{5,1},{6,2},{7,3},{8,4},{9,5},{10,6},{11,7},{12,8},{13,9},{1... | collective-permute-start | bytes 3145736 | tf_op jit(solution)/shard_map/ppermute | solution.py:23
  3.2 1.3 collective-permute-start.2
  5.2 1.5 %constant_dynamic-slice_fusion = (s32[1,1,1]{2,1,0:T(1,128)}, s32[1,1,1]{2,1,0:T(1,128)}, s32[1,1,1]{2,1,0:T(1,128)}, s32[1,1,1]{2,1,0:T(1,128)}) fusion(s32[1,2,2]{2,1,0:T(2,128)} %param.11, s32[]{:T(128)S(6)} %select_n.62, s32[]{:T(128)S(6)} %select_n.58), kind=kLoop, calls=%fused_computation.17 | loop fusion | bytes 40 | tf_op jit(solution)/shard_map/dynamic_slice | solution.py:253
  6.7 0.7 iota_compare_fusion.2
  7.4 0.7 iota_compare_fusion.3
  9.3 1.4 %pad_add_fusion.scalars = s32[4]{0:T(128)S(1)} fusion(s32[1]{0:T(128)} %bitcast.6, s32[1]{0:T(128)} %bitcast.5, s32[1]{0:T(128)} %bitcast.3, s32[1]{0:T(128)} %bitcast.2), kind=kLoop, calls=%fused_computation.22 | loop fusion | flops 12 | bytes 32 | tf_op jit(solution)/shard_map/stack | solution.py:260
  10.8 1.0 copy-done.4
  12.5 1.0 copy-done.6
  13.5 4.8 %tables.1 = (bf16[512,1536]{1,0:T(8,128)(2,1)S(1)}, bf16[512,1536]{1,0:T(8,128)(2,1)S(1)}, bf16[1536,512]{1,0:T(8,128)(2,1)S(1)}, bf16[1536,512]{1,0:T(8,128)(2,...) custom-call(s32[4]{0:T(128)S(1)} %pad_add_fusion.scalars, ...), custom_call_target="tpu_custom_call" | custom-call | flops 10000000000 | bytes 30000000 | tf_op jit(solution)/shard_map/tables/pallas_call | solution.py:202
  18.4 1.2 copy-done.2
  19.5 7.5 %collective-permute-done = f32[2,2,256,256]{3,2,1,0:T(8,128)S(1)} collective-permute-done((f32[2,2,256,256]{3,2,1,0:T(8,128)}, f32[2,2,256,256]{3,2,1,0:T(8,128)S(1)}, u32[]{:S(2)}, u32[]{:S(2)}) %collective-permute-start) | collective-permute-done | bytes 1048608 | tf_op jit(solution)/shard_map/ppermute | solution.py:23
  27.0 1.3 collective-permute-done.1
  28.3 24.3 %collective-permute-done.2 = f32[2,2,256,256]{3,2,1,0:T(8,128)S(1)} collective-permute-done((f32[2,2,256,256]{3,2,1,0:T(8,128)}, f32[2,2,256,256]{3,2,1,0:T(8,128)S(1)}, u32[]{:S(2)}, u32[]{:S(2)}) %collective-permute-start.2) | collective-permute-done | bytes 1048608 | tf_op jit(solution)/shard_map/ppermute | solution.py:23
  53.0 2.6 %collective-permute-done.3.other = f32[2,2,256,256]{3,2,1,0:T(8,128)S(1)} collective-permute-done((f32[2,2,256,256]{3,2,1,0:T(8,128)S(1)}, f32[2,2,256,256]{3,2,1,0:T(8,128)S(1)}, u32[]{:S(2)}, u32[]{:S(2)}) %collective-permute-start.3) | collective-permute-done | bytes 1048608 | tf_op jit(solution)/shard_map/ppermute | solution.py:27
  55.7 2.5 %wave.1 = (f32[2,2,256,256]{3,2,1,0:T(8,128)S(1)}, f32[2,2,256,256]{3,2,1,0:T(8,128)S(1)}) custom-call(s32[4]{0:T(128)S(1)} %pad_add_fusion.scalars, f32[2,2,256,256]{3,2,1,0:T(8,128)S(1)} %get-tuple-element.52.mine, f32[2,2,256,256]{3,2,1,0:T(8,128)S(1)} %collective-permute-done.3.other, f32[2,256,256]{2,1,0:T(8,128)S(1)} %get-tuple-element.40.probe, ...), custom_call_target="tpu_custom_call" | custom-call | tf_op jit(solution)/shard_map/wave/pallas_call | solution.py:226
  58.8 2.1 %collective-permute-done.4 = f32[2,2,256,256]{3,2,1,0:T(8,128)S(1)} collective-permute-done((f32[2,2,256,256]{3,2,1,0:T(8,128)S(1)}, f32[2,2,256,256]{3,2,1,0:T(8,128)S(1)}, u32[]{:S(2)}, u32[]{:S(2)}) %collective-permute-start.4) | collective-permute-done | bytes 1048608 | tf_op jit(solution)/shard_map/ppermute | solution.py:27
  61.4 4.4 %collective-permute-start.5 = (f32[2,2,256,256]{3,2,1,0:T(8,128)S(1)}, f32[2,2,256,256]{3,2,1,0:T(8,128)S(1)}, u32[]{:S(2)}, u32[]{:S(2)}) collective-permute-start(f32[2,2,256,256]{3,2,1,0:T(8,128)S(1)} %get-tuple-element.53), channel_id=1, source_target_pairs={{0,1},{1,2},{2,3},{4,5},{5,6},{6,7},{8,9},{9,10},{10,11},{12,13},{... | collective-permute-start | bytes 3145736 | tf_op jit(solution)/shard_map/ppermute | solution.py:23
  65.8 17.9 %collective-permute-start.6 = (f32[2,2,256,256]{3,2,1,0:T(8,128)S(1)}, f32[2,2,256,256]{3,2,1,0:T(8,128)S(1)}, u32[]{:S(2)}, u32[]{:S(2)}) collective-permute-start(f32[2,2,256,256]{3,2,1,0:T(8,128)S(1)} %get-tuple-element.55), channel_id=1, source_target_pairs={{0,4},{1,5},{2,6},{3,7},{4,8},{5,9},{6,10},{7,11},{8,12},{9,13},{1... | collective-permute-start | bytes 3145736 | tf_op jit(solution)/shard_map/ppermute | solution.py:23
  83.7 2.0 %collective-permute-start.7 = (f32[2,2,256,256]{3,2,1,0:T(8,128)S(1)}, f32[2,2,256,256]{3,2,1,0:T(8,128)S(1)}, u32[]{:S(2)}, u32[]{:S(2)}) collective-permute-start(f32[2,2,256,256]{3,2,1,0:T(8,128)S(1)} %get-tuple-element.54), channel_id=1, source_target_pairs={{0,5},{1,6},{2,7},{4,9},{5,10},{6,11},{8,13},{9,14},{10,15},{16,21... | collective-permute-start | bytes 3145736 | tf_op jit(solution)/shard_map/ppermute | solution.py:23
  85.8 2.7 %collective-permute-done.5 = f32[2,2,256,256]{3,2,1,0:T(8,128)S(1)} collective-permute-done((f32[2,2,256,256]{3,2,1,0:T(8,128)S(1)}, f32[2,2,256,256]{3,2,1,0:T(8,128)S(1)}, u32[]{:S(2)}, u32[]{:S(2)}) %collective-permute-start.5) | collective-permute-done | bytes 1048608 | tf_op jit(solution)/shard_map/ppermute | solution.py:23
  88.4 18.8 %collective-permute-done.6 = f32[2,2,256,256]{3,2,1,0:T(8,128)S(1)} collective-permute-done((f32[2,2,256,256]{3,2,1,0:T(8,128)S(1)}, f32[2,2,256,256]{3,2,1,0:T(8,128)S(1)}, u32[]{:S(2)}, u32[]{:S(2)}) %collective-permute-start.6) | collective-permute-done | bytes 1048608 | tf_op jit(solution)/shard_map/ppermute | solution.py:23
  107.3 21.3 %collective-permute-done.7 = f32[2,2,256,256]{3,2,1,0:T(8,128)S(1)} collective-permute-done((f32[2,2,256,256]{3,2,1,0:T(8,128)S(1)}, f32[2,2,256,256]{3,2,1,0:T(8,128)S(1)}, u32[]{:S(2)}, u32[]{:S(2)}) %collective-permute-start.7) | collective-permute-done | bytes 1048608 | tf_op jit(solution)/shard_map/ppermute | solution.py:23
  128.6 1.3 %add_bitcast_fusion = f32[2,2,1,256,256]{4,3,2,1,0:T(8,128)} fusion(f32[2,2,256,256]{3,2,1,0:T(8,128)S(1)} %collective-permute-done.7, f32[2,2,256,256]{3,2,1,0:T(8,128)S(1)} %collective-permute-done.6, f32[2,2,256,256]{3,2,1,0:T(8,128)S(1)} %collective-permute-done.5, f32[2,2,256,256]{3,2,1,0:T(8,128)S(1)} %collective-permute-done.4, ...), kind=kLoop, calls=%fused_computation | loop fusion | flops 1572864 | bytes 6422528 | tf_op jit(solution)/shard_map/broadcast_in_dim | solution.py:280
  (21 shorter events, 3.5 us)
Async XLA Ops:
  0.0 27.0 %collective-permute-start = (f32[2,2,256,256]{3,2,1,0:T(8,128)}, f32[2,2,256,256]{3,2,1,0:T(8,128)S(1)}, u32[]{:S(2)}, u32[]{:S(2)}) collective-permute-start(f32[2,2,256,256]{3,2,1,0:T(8,128)} %bitcast.19), channel_id=1, source_target_pairs={{1,0},{2,1},{3,2},{5,4},{6,5},{7,6},{9,8},{10,9},{11,10},{13,12},{... | collective-permute-start | bytes 3145736 | tf_op jit(solution)/shard_map/ppermute | solution.py:23
  1.3 27.0 %collective-permute-start.1 = (f32[2,2,256,256]{3,2,1,0:T(8,128)}, f32[2,2,256,256]{3,2,1,0:T(8,128)S(1)}, u32[]{:S(2)}, u32[]{:S(2)}) collective-permute-start(f32[2,2,256,256]{3,2,1,0:T(8,128)} %bitcast.20), channel_id=1, source_target_pairs={{4,0},{5,1},{6,2},{7,3},{8,4},{9,5},{10,6},{11,7},{12,8},{13,9},{1... | collective-permute-start | bytes 3145736 | tf_op jit(solution)/shard_map/ppermute | solution.py:23
  3.2 49.3 %collective-permute-start.2 = (f32[2,2,256,256]{3,2,1,0:T(8,128)}, f32[2,2,256,256]{3,2,1,0:T(8,128)S(1)}, u32[]{:S(2)}, u32[]{:S(2)}) collective-permute-start(f32[2,2,256,256]{3,2,1,0:T(8,128)} %bitcast.21), channel_id=1, source_target_pairs={{5,0},{6,1},{7,2},{9,4},{10,5},{11,6},{13,8},{14,9},{15,10},{21,16... | collective-permute-start | bytes 3145736 | tf_op jit(solution)/shard_map/ppermute | solution.py:23
  10.8 1.0 copy-start.4
  11.8 0.7 copy-start.5
  12.5 1.0 copy-start.6
  13.5 39.0 %copy-start.7 = (f32[2,2,1,256,256]{4,3,2,1,0:T(8,128)S(1)}, f32[2,2,1,256,256]{4,3,2,1,0:T(8,128)}, u32[]{:S(2)}) copy-start(f32[2,2,1,256,256]{4,3,2,1,0:T(8,128)} %param.7) | copy-start | bytes 3145732
  18.4 1.2 copy-start.2
  19.5 33.4 %copy-start = (bf16[512,1536]{1,0:T(8,128)(2,1)}, bf16[512,1536]{1,0:T(8,128)(2,1)S(1)}, u32[]{:S(2)}) copy-start(bf16[512,1536]{1,0:T(8,128)(2,1)S(1)} %get-tuple-element.46.far_lb) | copy-start | bytes 4718596
  19.5 33.4 %copy-start.1 = (bf16[1536,512]{1,0:T(8,128)(2,1)}, bf16[1536,512]{1,0:T(8,128)(2,1)S(1)}, u32[]{:S(2)}) copy-start(bf16[1536,512]{1,0:T(8,128)(2,1)S(1)} %get-tuple-element.47.far_rf) | copy-start | bytes 4718596
  52.6 3.1 %copy-start.3 = (f32[1,2,256,256]{3,2,1,0:T(8,128)S(1)}, f32[1,2,256,256]{3,2,1,0:T(8,128)}, u32[]{:S(2)}) copy-start(f32[1,2,256,256]{3,2,1,0:T(8,128)} %param.10) | copy-start | bytes 1572868
  53.0 2.7 %collective-permute-start.3 = (f32[2,2,256,256]{3,2,1,0:T(8,128)S(1)}, f32[2,2,256,256]{3,2,1,0:T(8,128)S(1)}, u32[]{:S(2)}, u32[]{:S(2)}) collective-permute-start(f32[2,2,256,256]{3,2,1,0:T(8,128)S(1)} %get-tuple-element.51), channel_id=1, source_target_pairs={{0,16},{16,0},{1,17},{17,1},{2,18},{18,2},{3,19},{19,3},{4,20},{20... | collective-permute-start | bytes 3145736 | tf_op jit(solution)/shard_map/ppermute | solution.py:27
  58.2 2.7 %collective-permute-start.4 = (f32[2,2,256,256]{3,2,1,0:T(8,128)S(1)}, f32[2,2,256,256]{3,2,1,0:T(8,128)S(1)}, u32[]{:S(2)}, u32[]{:S(2)}) collective-permute-start(f32[2,2,256,256]{3,2,1,0:T(8,128)S(1)} %get-tuple-element.50), channel_id=1, source_target_pairs={{0,16},{16,0},{1,17},{17,1},{2,18},{18,2},{3,19},{19,3},{4,20},{20... | collective-permute-start | bytes 3145736 | tf_op jit(solution)/shard_map/ppermute | solution.py:27
  61.4 27.0 %collective-permute-start.5 = (f32[2,2,256,256]{3,2,1,0:T(8,128)S(1)}, f32[2,2,256,256]{3,2,1,0:T(8,128)S(1)}, u32[]{:S(2)}, u32[]{:S(2)}) collective-permute-start(f32[2,2,256,256]{3,2,1,0:T(8,128)S(1)} %get-tuple-element.53), channel_id=1, source_target_pairs={{0,1},{1,2},{2,3},{4,5},{5,6},{6,7},{8,9},{9,10},{10,11},{12,13},{... | collective-permute-start | bytes 3145736 | tf_op jit(solution)/shard_map/ppermute | solution.py:23
  65.8 41.5 %collective-permute-start.6 = (f32[2,2,256,256]{3,2,1,0:T(8,128)S(1)}, f32[2,2,256,256]{3,2,1,0:T(8,128)S(1)}, u32[]{:S(2)}, u32[]{:S(2)}) collective-permute-start(f32[2,2,256,256]{3,2,1,0:T(8,128)S(1)} %get-tuple-element.55), channel_id=1, source_target_pairs={{0,4},{1,5},{2,6},{3,7},{4,8},{5,9},{6,10},{7,11},{8,12},{9,13},{1... | collective-permute-start | bytes 3145736 | tf_op jit(solution)/shard_map/ppermute | solution.py:23
  83.7 44.9 %collective-permute-start.7 = (f32[2,2,256,256]{3,2,1,0:T(8,128)S(1)}, f32[2,2,256,256]{3,2,1,0:T(8,128)S(1)}, u32[]{:S(2)}, u32[]{:S(2)}) collective-permute-start(f32[2,2,256,256]{3,2,1,0:T(8,128)S(1)} %get-tuple-element.54), channel_id=1, source_target_pairs={{0,5},{1,6},{2,7},{4,9},{5,10},{6,11},{8,13},{9,14},{10,15},{16,21... | collective-permute-start | bytes 3145736 | tf_op jit(solution)/shard_map/ppermute | solution.py:23
